TPU v7x, 128 devices: a whole 4x4x4 slice. The times are simulated.
128 devices in a mesh: seq: 8 (over y, core), chan: 16 (over z, x).
Axes of the slice: x: 4, y: 4, z: 4, core: 2. Of those that a mesh axis runs over, the one named last changes fastest.
Arguments:
- hidden: bfloat16 [1024, 4096], P('seq', 'chan'), may hold values from -6 to 6
- gate_in: bfloat16 [1024, 8192], P('seq', 'chan'), may hold values from -6 to 6
- out_grad: bfloat16 [1024, 8192], P('seq', 'chan'), may hold values from -6 to 6
- w_in: bfloat16 [4096, 8192], P('seq', 'chan'), may hold values from -0.125 to 0.125
- conv_w: float32 [4, 8192], P(None, 'chan'), may hold values from -2.5 to 2.5
- conv_b: float32 [8192], P('chan'), may hold values from -0.5 to 0.5
- w_delta_in: bfloat16 [256, 8192], P(None, 'chan'), may hold values from -0.0625 to 0.0625
- w_bc: bfloat16 [32, 8192], P(None, 'chan'), may hold values from -0.125 to 0.125
- w_dt: bfloat16 [256, 8192], P(None, 'chan'), may hold values from -0.375 to 0.375
- dt_bias: float32 [8192], P('chan'), may hold values from -7.5 to -2.5
- a_log: float32 [16, 8192], P(None, 'chan'), may hold values from -2.31 to 1.39
- skip_d: float32 [8192], P('chan'), may hold values from 0.1 to 1
Outputs:
- hidden_grad: bfloat16 [1024, 4096], P('seq', 'chan')
- gate_grad: bfloat16 [1024, 8192], P('seq', 'chan')
- w_in_grad: float32 [4096, 8192], P('seq', 'chan')
- w_delta_in_grad: float32 [256, 8192], P(None, 'chan')
- w_bc_grad: float32 [32, 8192], P(None, 'chan')
- w_dt_grad: float32 [256, 8192], P(None, 'chan')
- a_log_grad: float32 [16, 8192], P(None, 'chan')
All inputs are finite; a program needn't handle non-finite values.
Results may differ from a plain program's by a relative error of at most 0.035.
Values may be sent and summed in bfloat16 or wider, within the bound.
A program may use at most 64 MiB of HBM per device.

v0:
```python
import math

import jax
import jax.numpy as jnp
from jax import lax
from jax.sharding import PartitionSpec as P

BLK = 64


def entering(shard, axis, join, neutral):
    place = lax.axis_index(axis)
    gathered = jax.tree.map(
        lambda a, kind: lax.all_gather(a.astype(kind), axis), shard, (jnp.bfloat16, jnp.bfloat16)
    )
    state = jax.tree.map(lambda a, e: jnp.zeros_like(a) + jnp.asarray(e, a.dtype), shard, neutral)

    def one(turn, state):
        return join(
            state,
            jax.tree.map(
                lambda a, own: lax.dynamic_index_in_dim(a, turn, 0, False).astype(own.dtype),
                gathered,
                shard,
            ),
        )

    return lax.fori_loop(0, place, one, state)


def prefix(shard, axis, combine, identity):
    count, place = (lax.axis_size(axis), lax.axis_index(axis))
    everything = jax.tree.map(
        lambda part, kind: lax.all_gather(part.astype(kind), axis),
        shard,
        jax.tree.map(lambda a: jnp.bfloat16 if a.dtype == jnp.float32 else a.dtype, shard),
    )
    start = jax.tree.map(
        lambda part, zero: jnp.broadcast_to(jnp.asarray(zero, part.dtype), part.shape),
        shard,
        identity,
    )

    def turn(k, before):
        at = count - 1 - k
        reached = at > place
        new = combine(
            before, jax.tree.map(lambda part, own: part[at].astype(own.dtype), everything, shard)
        )
        return jax.tree.map(lambda a, b: jnp.where(reached, a, b), new, before)

    return lax.fori_loop(0, count, turn, start)


def from_behind(block, axis, distance):
    devices = range(lax.axis_size(axis))
    route = [(i - distance, i) for i in devices if i - distance in devices]
    return lax.ppermute(block, axis, route)


def chain_pair(earlier, later):
    return (earlier[0] * later[0], later[0] * earlier[1] + later[1])


def silu_slope(values):
    sig = jax.nn.sigmoid(values)
    return sig * (1.0 + values * (1.0 - sig))


def local_scan(u_float, delta, b_in, c_in, a_matrix, state_in):
    tokens, chans = u_float.shape
    states = a_matrix.shape[0]
    blocks = tokens // BLK

    def token_step(state, row):
        u_row, d_row, b_row, c_row = row
        state = (
            jnp.exp(d_row[None, :] * a_matrix) * state + (d_row * u_row)[None, :] * b_row[:, None]
        )
        return (state, jnp.sum(c_row[:, None] * state, 0))

    def step(carried, pieces):
        return lax.scan(token_step, carried, pieces, unroll=8)

    pieces = (
        u_float.reshape(blocks, BLK, chans),
        delta.reshape(blocks, BLK, chans),
        b_in.reshape(blocks, BLK, states),
        c_in.reshape(blocks, BLK, states),
    )
    final_state, outputs = lax.scan(jax.checkpoint(step), state_in, pieces)
    return (outputs.reshape(tokens, chans), final_state)


def contract_last(left, right):
    return lax.dot_general(
        left, right, (((1,), (1,)), ((), ())), preferred_element_type=jnp.float32
    )


def contract_first(left, right):
    return lax.dot_general(
        left, right, (((0,), (0,)), ((), ())), preferred_element_type=jnp.float32
    )


def carry_states(decays, finals, identity):
    return entering((decays, finals), "seq", chain_pair, identity)[1]


def carry_adjoint(decays, entries, identity):
    return prefix((decays, entries), "seq", chain_pair, identity)[1]


def per_device(
    hidden, gate_in, out_grad, w_in, conv_w, conv_b, w_delta_in, w_bc, w_dt, dt_bias, a_log, skip_d
):
    tokens = hidden.shape[0]
    chans = w_in.shape[1]
    kernel_len = conv_w.shape[0]
    states = a_log.shape[0]
    grad_scale = 1.0 / math.sqrt(tokens * lax.axis_size("seq"))
    whole = lax.all_gather(hidden, "chan", axis=1, tiled=True)
    columns = whole
    x_value = jnp.dot(
        columns, lax.all_gather(w_in, "seq", axis=0, tiled=True), preferred_element_type=jnp.float32
    )
    x_rounded = x_value.astype(jnp.bfloat16)
    tail_rows = from_behind(x_rounded[tokens - (kernel_len - 1) :], "seq", 1)
    padded = jnp.concatenate([tail_rows, x_rounded], 0).astype(jnp.float32)
    conv_pre = jnp.zeros((tokens, chans), jnp.float32) + conv_b
    for k in range(kernel_len):
        conv_pre = conv_pre + conv_w[k] * padded[k : k + tokens]
    u_rounded = jax.nn.silu(conv_pre).astype(jnp.bfloat16)
    low_summed, bc_summed = (
        lax.psum(contract_last(u_rounded, w_delta_in).astype(jnp.bfloat16), "chan").astype(
            jnp.float32
        ),
        lax.psum(contract_last(u_rounded, w_bc).astype(jnp.bfloat16), "chan").astype(jnp.float32),
    )
    dt_low = low_summed.astype(jnp.bfloat16)
    b_in = bc_summed[:, :states]
    c_in = bc_summed[:, states:]
    pre_delta = jnp.dot(dt_low, w_dt, preferred_element_type=jnp.float32) + dt_bias
    delta = jax.nn.softplus(pre_delta)
    a_matrix = -jnp.exp(a_log)
    u_float = u_rounded.astype(jnp.float32)
    gate_float = gate_in.astype(jnp.float32)
    grad_float = out_grad.astype(jnp.float32)
    y_adj = grad_float * jax.nn.silu(gate_float)
    block_decay = jnp.exp(a_matrix * jnp.sum(delta, 0)[None])
    zero_state = jnp.zeros((states, chans), jnp.float32)
    identity = (jnp.ones_like(zero_state), zero_state)
    free_end = local_scan(u_float, delta, b_in, c_in, a_matrix, zero_state)[1]
    start_state = carry_states(block_decay, free_end, identity)
    (scan_out, final_state), backward = jax.vjp(
        local_scan, u_float, delta, b_in, c_in, a_matrix, start_state
    )
    front_part = backward((y_adj, zero_state))
    end_adj = carry_adjoint(block_decay, front_part[5], identity)
    second = backward((jnp.zeros_like(y_adj), end_adj))
    u_scan_adj = front_part[0] + second[0]
    delta_adj = front_part[1] + second[1]
    b_adj = front_part[2] + second[2]
    c_adj = front_part[3] + second[3]
    a_adj = front_part[4] + second[4]
    y_out = scan_out + skip_d * u_float
    gate_grad = (grad_float * y_out * silu_slope(gate_float)).astype(jnp.bfloat16)
    pre_adj = (delta_adj * jax.nn.sigmoid(pre_delta)).astype(jnp.bfloat16)
    low_part = contract_last(pre_adj, w_dt)
    bc_part = jnp.concatenate([b_adj, c_adj], 1)
    low_total, bc_total = (
        lax.psum(low_part.astype(jnp.bfloat16), "chan").astype(jnp.float32),
        lax.psum(bc_part.astype(jnp.bfloat16), "chan").astype(jnp.float32),
    )
    low_adj = low_total.astype(jnp.bfloat16)
    bc_adj = bc_total.astype(jnp.bfloat16)
    u_adj = (
        u_scan_adj
        + skip_d * y_adj
        + jnp.dot(low_adj, w_delta_in, preferred_element_type=jnp.float32)
        + jnp.dot(bc_adj, w_bc, preferred_element_type=jnp.float32)
    )
    conv_adj = u_adj * silu_slope(conv_pre)
    head_rows = from_behind(conv_adj[: kernel_len - 1], "seq", -1)
    padded_back = jnp.concatenate([conv_adj, head_rows], 0)
    x_adj = jnp.zeros((tokens, chans), jnp.float32)
    for k in range(kernel_len):
        x_adj = x_adj + conv_w[k] * padded_back[kernel_len - 1 - k : kernel_len - 1 - k + tokens]
    x_adj = x_adj.astype(jnp.bfloat16)
    partial_in = contract_last(x_adj, lax.all_gather(w_in, "seq", axis=0, tiled=True))
    hidden_grad = lax.psum_scatter(
        partial_in.astype(jnp.bfloat16), "chan", scatter_dimension=1, tiled=True
    )
    columns = whole
    w_in_grad = (
        lax.psum_scatter(
            contract_first(columns, x_adj).astype(jnp.bfloat16),
            "seq",
            scatter_dimension=0,
            tiled=True,
        ).astype(jnp.float32)
        * grad_scale
    )
    delta_in_term = contract_first(low_adj, u_rounded)
    bc_term = contract_first(bc_adj, u_rounded)
    dt_term = contract_first(dt_low, pre_adj)
    rate_term = a_adj * a_matrix
    delta_in_sum, bc_sum, dt_sum, rate_sum = (
        lax.psum(delta_in_term.astype(jnp.bfloat16), "seq").astype(jnp.float32),
        lax.psum(bc_term.astype(jnp.bfloat16), "seq").astype(jnp.float32),
        lax.psum(dt_term.astype(jnp.bfloat16), "seq").astype(jnp.float32),
        lax.psum(rate_term.astype(jnp.bfloat16), "seq").astype(jnp.float32),
    )
    return (
        hidden_grad,
        gate_grad,
        w_in_grad,
        delta_in_sum * grad_scale,
        bc_sum * grad_scale,
        dt_sum * grad_scale,
        rate_sum * grad_scale,
    )


def solution(mesh):
    placed = (
        P("seq", "chan"),
        P("seq", "chan"),
        P("seq", "chan"),
        P("seq", "chan"),
        P(None, "chan"),
        P("chan"),
        P(None, "chan"),
        P(None, "chan"),
        P(None, "chan"),
        P("chan"),
        P(None, "chan"),
        P("chan"),
    )
    return jax.shard_map(
        per_device,
        mesh=mesh,
        in_specs=placed,
        out_specs=(
            P("seq", "chan"),
            P("seq", "chan"),
            P("seq", "chan"),
            P(None, "chan"),
            P(None, "chan"),
            P(None, "chan"),
            P(None, "chan"),
        ),
        check_vma=False,
    )
```

profile of v0, /device:TPU:1, one launch (start us, length us, event | category | flops | bytes accessed | tf_op | source)
XLA Modules:
  0.0 794.2 jit_solution(4651613737092170675)
XLA Ops:
  9.8 45.7 %all-gather.6.cloned.1.call-done = bf16[128,4096]{1,0:T(8,128)(2,1)} async-done(((bf16[128,256]{1,0:T(8,128)(2,1)}), bf16[128,4096]{1,0:T(8,128)(2,1)}) %all-gather.6.cloned.1.call-update) | async-done | bytes 1048592 | tf_op jit(solution)/shard_map/all_gather | solution.py:123
  55.5 34.9 %all-gather.8.cloned.1.call-done = bf16[4096,512]{1,0:T(8,128)(2,1)} async-done(((bf16[512,512]{1,0:T(8,128)(2,1)}), bf16[4096,512]{1,0:T(8,128)(2,1)}) %all-gather.8.cloned.1.call-update) | async-done | bytes 4194320 | tf_op jit(solution)/shard_map/all_gather | solution.py:126
  98.9 33.9 %psum.57 = bf16[128,32]{0,1:T(8,128)(2,1)S(1)} all-reduce(bf16[128,32]{0,1:T(8,128)(2,1)S(1)} %convolution_convert_fusion.8), channel_id=1, replica_groups=mesh['seq'=8,'chan'=16] {'chan'}, use_global_device_ids=true, to_apply=%region_2.3 | all-reduce | flops 4096 | bytes 16384 | tf_op jit(solution)/shard_map/psum | solution.py:139
  133.0 46.6 %all-reduce.6.cloned.1.call-done = bf16[128,256]{1,0:T(8,128)(2,1)} async-done(((bf16[128,256]{1,0:T(8,128)(2,1)}), bf16[128,256]{1,0:T(8,128)(2,1)}) %all-reduce.6.cloned.1.call-update) | async-done | bytes 65552 | tf_op jit(solution)/shard_map/psum | solution.py:136
  186.6 15.1 %all-gather.1 = bf16[128,512]{1,0:T(8,128)(2,1)S(1)} all-gather(bf16[16,512]{1,0:T(8,128)(2,1)S(1)} %convert_element_type.140), channel_id=3, replica_groups=mesh['seq'=8,'chan'=16] {'seq'}, dimensions={0}, use_global_device_ids=true | all-gather | bytes 147456 | tf_op jit(solution)/shard_map/all_gather | solution.py:14
  201.7 12.7 %all-gather = bf16[128,512]{1,0:T(8,128)(2,1)S(1)} all-gather(bf16[16,512]{1,0:T(8,128)(2,1)S(1)} %get-tuple-element.3158), channel_id=2, replica_groups=mesh['seq'=8,'chan'=16] {'seq'}, dimensions={0}, use_global_device_ids=true | all-gather | bytes 147456 | tf_op jit(solution)/shard_map/all_gather | solution.py:14
  215.2 10.7 %while.358 = (s32[]{:T(128)}, f32[16,512]{1,0:T(8,128)S(1)}, f32[2,64,512]{2,1,0:T(8,128)S(1)}, f32[2,16,512]{2,1,0:T(8,128)S(1)}, f32[2,64,512]{2,1,0:T(8,128)S...) while((s32[]{:T(128)}, f32[16,512]{1,0:T(8,128)S(1)}, ...), condition=%wide.region_20.21_spmd, body=%wide.region_9.20_spmd.sunk | while | flops 589835 | bytes 1521646 | solution.py:91
  227.9 118.9 %while.361 = (s32[]{:T(128)}, f32[16,512]{1,0:T(8,128)S(1)}, f32[16,512]{1,0:T(8,128)S(1)}, f32[2,64,512]{2,1,0:T(8,128)S(1)}, f32[2,64,512]{2,1,0:T(8,128)}, /*...) while((s32[]{:T(128)}, f32[16,512]{1,0:T(8,128)S(1)}, ...), condition=%wide.region_58.59_spmd.clone, body=%wide.region_21.58_spmd.clone.sunk | while | flops 1494805 | bytes 7908439 | solution.py:91
  228.1 23.1 %while.368 = (s32[]{:T(128)}, f32[16,512]{1,0:T(8,128)S(1)}, f32[8,8,16,512]{3,2,1,0:T(8,128)}, f32[8,8,16,1]{2,1,3,0:T(8,128)S(1)}, f32[8,8,1,512]{3,2,1,0:T(1,...) while((s32[]{:T(128)}, f32[16,512]{1,0:T(8,128)S(1)}, ...), condition=%wide.region_23.23_spmd, body=%wide.region_22.22_spmd.sunk | while | flops 466950 | bytes 3417581 | solution.py:83
  251.3 35.3 %while.369 = (s32[]{:T(128)}, f32[16,512]{1,0:T(8,128)S(1)}, f32[16,512]{1,0:T(8,128)S(1)}, f32[8,8,512]{2,1,0:T(8,128)S(1)}, f32[8,8,512]{2,1,0:T(8,128)S(1)}, ...) while((s32[]{:T(128)}, f32[16,512]{1,0:T(8,128)S(1)}, ...), condition=%wide.region_57.57_spmd.clone, body=%wide.region_24.56_spmd.clone.sunk | while | flops 1011467 | bytes 2466519 | solution.py:83
  287.6 23.1 %while.368 = (s32[]{:T(128)}, f32[16,512]{1,0:T(8,128)S(1)}, f32[8,8,16,512]{3,2,1,0:T(8,128)}, f32[8,8,16,1]{2,1,3,0:T(8,128)S(1)}, f32[8,8,1,512]{3,2,1,0:T(1,...) while((s32[]{:T(128)}, f32[16,512]{1,0:T(8,128)S(1)}, ...), condition=%wide.region_23.23_spmd, body=%wide.region_22.22_spmd.sunk | while | flops 466950 | bytes 3417581 | solution.py:83
  310.8 35.3 %while.369 = (s32[]{:T(128)}, f32[16,512]{1,0:T(8,128)S(1)}, f32[16,512]{1,0:T(8,128)S(1)}, f32[8,8,512]{2,1,0:T(8,128)S(1)}, f32[8,8,512]{2,1,0:T(8,128)S(1)}, ...) while((s32[]{:T(128)}, f32[16,512]{1,0:T(8,128)S(1)}, ...), condition=%wide.region_57.57_spmd.clone, body=%wide.region_24.56_spmd.clone.sunk | while | flops 1011467 | bytes 2466519 | solution.py:83
  346.9 12.7 %all-gather.2 = bf16[128,512]{1,0:T(8,128)(2,1)S(1)} all-gather(bf16[16,512]{1,0:T(8,128)(2,1)S(1)} %convert_element_type.143), channel_id=4, replica_groups=mesh['seq'=8,'chan'=16] {'seq'}, dimensions={0}, use_global_device_ids=true | all-gather | bytes 147456 | tf_op jit(solution)/shard_map/all_gather | solution.py:34
  368.4 120.0 %while.365 = (s32[]{:T(128)}, f32[16,512]{1,0:T(8,128)S(1)}, f32[16,512]{1,0:T(8,128)S(1)}, f32[2,64,512]{2,1,0:T(8,128)}, f32[2,64,512]{2,1,0:T(8,128)}, /*inde...) while((s32[]{:T(128)}, f32[16,512]{1,0:T(8,128)S(1)}, ...), condition=%wide.region_98.99_spmd.clone, body=%wide.region_61.98_spmd.clone.sunk | while | flops 1494805 | bytes 7588831 | solution.py:91
  368.5 23.1 %while.370 = (s32[]{:T(128)}, f32[16,512]{1,0:T(8,128)S(1)}, f32[8,8,16,512]{3,2,1,0:T(8,128)}, f32[8,8,16,1]{2,1,3,0:T(8,128)S(1)}, f32[8,8,1,512]{3,2,1,0:T(1,...) while((s32[]{:T(128)}, f32[16,512]{1,0:T(8,128)S(1)}, ...), condition=%wide.region_63.63_spmd, body=%wide.region_62.62_spmd.sunk | while | flops 466950 | bytes 3417581 | solution.py:83
  391.7 35.3 %while.371 = (s32[]{:T(128)}, f32[16,512]{1,0:T(8,128)S(1)}, f32[16,512]{1,0:T(8,128)S(1)}, f32[8,8,512]{2,1,0:T(8,128)S(1)}, f32[8,8,512]{2,1,0:T(8,128)S(1)}, ...) while((s32[]{:T(128)}, f32[16,512]{1,0:T(8,128)S(1)}, ...), condition=%wide.region_97.97_spmd.clone, body=%wide.region_64.96_spmd.clone.sunk | while | flops 1011467 | bytes 2466519 | solution.py:83
  428.5 23.1 %while.370 = (s32[]{:T(128)}, f32[16,512]{1,0:T(8,128)S(1)}, f32[8,8,16,512]{3,2,1,0:T(8,128)}, f32[8,8,16,1]{2,1,3,0:T(8,128)S(1)}, f32[8,8,1,512]{3,2,1,0:T(1,...) while((s32[]{:T(128)}, f32[16,512]{1,0:T(8,128)S(1)}, ...), condition=%wide.region_63.63_spmd, body=%wide.region_62.62_spmd.sunk | while | flops 466950 | bytes 3417581 | solution.py:83
  451.7 35.3 %while.371 = (s32[]{:T(128)}, f32[16,512]{1,0:T(8,128)S(1)}, f32[16,512]{1,0:T(8,128)S(1)}, f32[8,8,512]{2,1,0:T(8,128)S(1)}, f32[8,8,512]{2,1,0:T(8,128)S(1)}, ...) while((s32[]{:T(128)}, f32[16,512]{1,0:T(8,128)S(1)}, ...), condition=%wide.region_97.97_spmd.clone, body=%wide.region_64.96_spmd.clone.sunk | while | flops 1011467 | bytes 2466519 | solution.py:83
  489.6 31.5 %psum.59 = bf16[128,32]{0,1:T(8,128)(2,1)S(1)} all-reduce(bf16[128,32]{0,1:T(8,128)(2,1)S(1)} %pad_maximum_fusion.1), channel_id=1, replica_groups=mesh['seq'=8,'chan'=16] {'chan'}, use_global_device_ids=true, to_apply=%region_100.101 | all-reduce | flops 4096 | bytes 16384 | tf_op jit(solution)/shard_map/psum | solution.py:174
  526.2 79.9 %all-reduce.8.cloned.1.call-done = bf16[128,256]{1,0:T(8,128)(2,1)} async-done(((bf16[128,256]{1,0:T(8,128)(2,1)}), bf16[128,256]{1,0:T(8,128)(2,1)}) %all-reduce.8.cloned.1.call-update) | async-done | bytes 65552 | tf_op jit(solution)/shard_map/psum | solution.py:173
  622.3 23.0 %all-reduce = (bf16[32,512]{1,0:T(8,128)(2,1)S(1)}, bf16[16,512]{1,0:T(8,128)(2,1)S(1)}) all-reduce(bf16[32,512]{1,0:T(8,128)(2,1)S(1)} %convolution_convert_fusion.7, bf16[16,512]{1,0:T(8,128)(2,1)S(1)} %multiply_convert_fusion.1), channel_id=1, replica_groups=mesh['seq'=8,'chan'=16] {'seq'}, use_global_device_ids=true, to_apply=%region_104.105 | all-reduce | flops 24576 | bytes 98304 | tf_op jit(solution)/shard_map/psum | solution.py:211
  646.6 24.8 %all-reduce.10.cloned.1.call-done = (bf16[256,512]{1,0:T(8,128)(2,1)}, bf16[256,512]{1,0:T(8,128)(2,1)}) async-done(((bf16[256,512]{1,0:T(8,128)(2,1)}, bf16[256,512]{1,0:T(8,128)(2,1)}), (bf16[256,512]{1,0:T(8,128)(2,1)}, bf16[256,512]{1,0:T(8,128)(2,1)})) %all-reduce.10.cloned.1.call-update) | async-done | bytes 524304 | tf_op jit(solution)/shard_map/psum | solution.py:210
  673.5 36.4 %reduce-scatter.5.cloned.1.call-done = bf16[512,512]{0,1:T(8,128)(2,1)} async-done(((bf16[4096,512]{0,1:T(8,128)(2,1)}), bf16[512,512]{0,1:T(8,128)(2,1)}) %reduce-scatter.5.cloned.1.call-update) | async-done | bytes 524304 | tf_op jit(solution)/shard_map/reduce_scatter | solution.py:197
  712.4 75.0 %reduce-scatter.3.cloned.1.call-done = bf16[128,256]{1,0:T(8,128)(2,1)} async-done(((bf16[128,4096]{1,0:T(8,128)(2,1)}), bf16[128,256]{1,0:T(8,128)(2,1)}) %reduce-scatter.3.cloned.1.call-update) | async-done | bytes 65552 | tf_op jit(solution)/shard_map/reduce_scatter | solution.py:192
  (3278 shorter events, 317.6 us)
Async XLA Ops:
  7.2 172.4 %copy-start = (bf16[256,512]{1,0:T(8,128)(2,1)S(1)}, bf16[256,512]{1,0:T(8,128)(2,1)}, u32[]{:S(2)}) copy-start(bf16[256,512]{1,0:T(8,128)(2,1)} %param.44) | copy-start | bytes 786436
  7.2 48.3 %all-gather.6.cloned.1.call-start = ((), (), s32[]{:S(2)}) async-start(), calls=%async_computation.2 | async-start | bytes 1114112 | tf_op jit(solution)/shard_map/all_gather | solution.py:123
  7.9 82.5 %all-gather.8.cloned.1.call-start = ((), (), s32[]{:S(2)}) async-start(), calls=%async_computation.3 | async-start | bytes 4718592 | tf_op jit(solution)/shard_map/all_gather | solution.py:126
  8.7 170.9 %all-reduce.6.cloned.1.call-start = ((), (), s32[]{:S(2)}) async-start(), calls=%async_computation.4 | async-start | bytes 131072 | tf_op jit(solution)/shard_map/psum | solution.py:136
  9.8 86.3 %copy-start.23 = (f32[4,512]{1,0:T(4,128)S(1)}, f32[4,512]{1,0:T(4,128)}, u32[]{:S(2)}) copy-start(f32[4,512]{1,0:T(4,128)} %param.40) | copy-start | bytes 24580
  9.8 87.1 %copy-start.24 = (f32[512]{0:T(512)S(1)}, f32[512]{0:T(512)}, u32[]{:S(2)}) copy-start(f32[512]{0:T(512)} %param.41) | copy-start | bytes 6148
  9.8 88.0 %copy-start.9 = (bf16[256,512]{1,0:T(8,128)(2,1)S(1)}, bf16[256,512]{1,0:T(8,128)(2,1)}, u32[]{:S(2)}) copy-start(bf16[256,512]{1,0:T(8,128)(2,1)} %param.42) | copy-start | bytes 786436
  93.6 86.0 %copy-start.26 = (f32[512]{0:T(512)S(1)}, f32[512]{0:T(512)}, u32[]{:S(2)}) copy-start(f32[512]{0:T(512)} %param.45) | copy-start | bytes 6148
  93.7 87.8 %copy-start.16 = (f32[16,512]{1,0:T(8,128)S(1)}, f32[16,512]{1,0:T(8,128)}, u32[]{:S(2)}) copy-start(f32[16,512]{1,0:T(8,128)} %param.46) | copy-start | bytes 98308
  93.7 3.2 collective-permute-start
  96.1 85.4 %copy-start.19 = (f32[1,512]{1,0:T(1,128)}, f32[1,512]{1,0:T(1,128)S(1)}, u32[]{:S(2)}) copy-start(f32[1,512]{1,0:T(1,128)S(1)} %get-tuple-element.3163) | copy-start | bytes 6148
  96.1 85.4 %copy-start.21 = (f32[1,512]{1,0:T(1,128)}, f32[1,512]{1,0:T(1,128)S(1)}, u32[]{:S(2)}) copy-start(f32[1,512]{1,0:T(1,128)S(1)} %get-tuple-element.3164) | copy-start | bytes 6148
  98.7 507.4 %all-reduce.8.cloned.1.call-start = ((), (), s32[]{:S(2)}) async-start(), calls=%async_computation.5 | async-start | bytes 131072 | tf_op jit(solution)/shard_map/psum | solution.py:173
  368.4 120.0 %copy-start.12 = (f32[2,64,16]{2,1,0:T(8,128)S(1)}, f32[2,64,16]{2,1,0:T(8,128)}, u32[]{:S(2)}) copy-start(f32[2,64,16]{2,1,0:T(8,128)} %get-tuple-element.1959) | copy-start | bytes 24580
  368.4 152.7 %copy-start.2 = (f32[2,64,512]{2,1,0:T(8,128)S(1)}, f32[2,64,512]{2,1,0:T(8,128)}, u32[]{:S(2)}) copy-start(f32[2,64,512]{2,1,0:T(8,128)} %get-tuple-element.1957) | copy-start | bytes 786436
  488.4 35.8 %copy-start.5 = (f32[2,64,512]{2,1,0:T(8,128)S(1)}, f32[2,64,512]{2,1,0:T(8,128)}, u32[]{:S(2)}) copy-start(f32[2,64,512]{2,1,0:T(8,128)} %copy-done.4) | copy-start | bytes 786436
  488.4 35.8 %copy-start.7 = (bf16[128,512]{1,0:T(8,128)(2,1)S(1)}, bf16[128,512]{1,0:T(8,128)(2,1)}, u32[]{:S(2)}) copy-start(bf16[128,512]{1,0:T(8,128)(2,1)} %param.38) | copy-start | bytes 393220
  524.0 147.3 %all-reduce.10.cloned.1.call-start = ((), (), s32[]{:S(2)}) async-start(), calls=%async_computation.8 | async-start | bytes 1048576 | tf_op jit(solution)/shard_map/psum | solution.py:210
  524.2 89.8 %copy-start.20 = (f32[1,512]{1,0:T(1,128)S(1)}, f32[1,512]{1,0:T(1,128)}, u32[]{:S(2)}) copy-start(f32[1,512]{1,0:T(1,128)} %copy-done.19) | copy-start | bytes 6148
  524.2 89.7 %copy-start.22 = (f32[1,512]{1,0:T(1,128)S(1)}, f32[1,512]{1,0:T(1,128)}, u32[]{:S(2)}) copy-start(f32[1,512]{1,0:T(1,128)} %copy-done.21) | copy-start | bytes 6148
  525.0 89.0 %copy-start.1 = (bf16[128,4096]{1,0:T(8,128)(2,1)S(1)}, bf16[128,4096]{1,0:T(8,128)(2,1)}, u32[]{:S(2)}) copy-start(bf16[128,4096]{1,0:T(8,128)(2,1)} %all-gather.6.cloned.1.call-done) | copy-start | bytes 3145732
  607.4 6.6 collective-permute-start.1
  613.3 96.5 %reduce-scatter.5.cloned.1.call-start = ((), (), s32[]{:S(2)}) async-start(), calls=%async_computation.7 | async-start | bytes 4718592 | tf_op jit(solution)/shard_map/reduce_scatter | solution.py:197
  617.4 170.0 %reduce-scatter.3.cloned.1.call-start = ((), (), s32[]{:S(2)}) async-start(), calls=%async_computation.6 | async-start | bytes 1114112 | tf_op jit(solution)/shard_map/reduce_scatter | solution.py:192
  (16 other events, 299.7 us)
Sparse Core Ops, SparseCore 0:
  10.1 45.2 all-gather.5
  57.2 33.1 all-gather.7
  98.8 80.7 all-reduce.5
  524.2 81.8 all-reduce.7
  613.5 57.8 all-reduce.9
  673.7 36.0 reduce-scatter.4
  714.0 73.3 reduce-scatter.2
where the time goes:
time: 803 us; the launch traced here: 794 us
  waiting for transfers between devices  346 us (43%)
  other arithmetic  178 us (22%)
  blocking collectives  129 us (16%)
  local copies, waits for them, and re-layouts  84.2 us (10%)
  matrix products  19.2 us (2%)
  loops' own time  16.1 us (2%)
  between operations  14.7 us (2%)
    psum x1, waiting for transfers between devices, per_device(): lax.psum(low_part.astype(jnp.bfloat16), 'chan').astype(jnp.float32)  79.9 us
    reduce_scatter x1, waiting for transfers between devices, per_device(): lax.psum_scatter(partial_in.astype(jnp.bfloat16), 'chan', scatter_dimensi...  75 us
    dynamic_update_slice x272, local copies, waits for them, and re-layouts, step(): return lax.scan(token_step, carried, pieces, unroll=8)  52.6 us
    psum x1, waiting for transfers between devices, per_device(): lax.psum(contract_last(u_rounded, w_delta_in).astype(jnp.bfloat16), 'chan')  46.6 us
    all_gather x1, waiting for transfers between devices, per_device(): whole = lax.all_gather(hidden, 'chan', axis=1, tiled=True)  45.7 us
    reduce_sum x128, other arithmetic, token_step(): (d_row * u_row)[None, :] * b_row[:, None]  44.6 us
    reduce_sum x80, other arithmetic, token_step(): return (state, jnp.sum(c_row[:, None] * state, 0))  42.6 us
    reduce_sum x32, other arithmetic, token_step(): d_row[None, :] * a_matrix  41.2 us
  transfers between devices with their start and end apart: 9, of which 9 were waited for; matrix products, arithmetic and copies ran while one was open for 2% of the time, Pallas kernels for 0%

commit v1 on v0

v1 whole, which is shorter than its diff:
```python
import functools
import math
import types

import jax
import jax.numpy as jnp
from jax import lax
from jax.experimental import pallas as pl
from jax.experimental.pallas import tpu as pltpu
from jax.sharding import PartitionSpec as P

MESH = pl.DeviceIdType.MESH


class Names:
    def __getattr__(self, name):
        return name


b = Names()
F32, BF16 = jnp.float32, jnp.bfloat16
CH = 16
LANES = 128
HALO = 16
HEAD = 8


def contract_last(left, right):
    return lax.dot_general(left, right, (((1,), (1,)), ((), ())), preferred_element_type=F32)


def contract_first(left, right):
    return lax.dot_general(left, right, (((0,), (0,)), ((), ())), preferred_element_type=F32)


def dot(left, right):
    return jnp.dot(left, right, preferred_element_type=F32)


def silu_slope(values):
    sig = jax.nn.sigmoid(values)
    return sig * (1.0 + values * (1.0 - sig))


def softplus(v):
    return jnp.maximum(v, 0.0) + jnp.log1p(jnp.exp(-jnp.abs(v)))


def rcopy(src, dst, send, recv, seq, chan):
    return pltpu.make_async_remote_copy(
        src_ref=src,
        dst_ref=dst,
        send_sem=send,
        recv_sem=recv,
        device_id=dict(seq=seq, chan=chan),
        device_id_type=MESH,
    )


def ring(r, group):
    if group == b.seq:
        return r.s, r.nS, lambda j: (j, r.c)
    return r.c, r.nC, lambda j: (r.s, j)


def peers(r, group):
    me, n, dev = ring(r, group)
    for i in range(1, n):
        j = lax.rem(me + i, n)
        yield i, j, dev(j)


def scatter_start(r, group, src, dst, key):
    me = ring(r, group)[0]
    for i, j, dev in peers(r, group):
        rcopy(src.at[j], dst.at[me], r.sems[key + "_s"].at[i], r.sems[key + "_r"].at[me], *dev).start()


def gather_start(r, group, buf, key):
    me = ring(r, group)[0]
    for i, j, dev in peers(r, group):
        rcopy(buf.at[me], buf.at[me], r.sems[key + "_s"].at[i], r.sems[key + "_r"].at[me], *dev).start()


def recv_wait(r, group, buf, key):
    for i, j, dev in peers(r, group):
        rcopy(buf.at[j], buf.at[j], r.sems[key + "_s"].at[i], r.sems[key + "_r"].at[j], *dev).wait_recv()


def send_wait(r, group, buf, key):
    for i, j, dev in peers(r, group):
        rcopy(buf.at[j], buf.at[j], r.sems[key + "_s"].at[i], r.sems[key + "_r"].at[j], *dev).wait_send()


def scatter_sum(r, group, src, dst, key):
    me = ring(r, group)[0]
    total = src[me].astype(F32)
    recv_wait(r, group, dst, key)
    for i, j, dev in peers(r, group):
        total = total + dst[j].astype(F32)
    return total


def greet(r, groups):
    barrier = pltpu.get_barrier_semaphore()
    count = 0

    def tell(seq, chan):
        pl.semaphore_signal(barrier, inc=1, device_id=dict(seq=seq, chan=chan), device_id_type=MESH)

    for group in groups:
        if group in (b.seq, b.chan):
            for i, j, dev in peers(r, group):
                tell(*dev)
                count += 1
        elif group == b.pair:
            tell(r.y * 2 + 1 - r.k, r.c)
            count += 1
        elif group == b.line:
            for i in range(1, r.nY):
                tell(lax.rem(r.y + i, r.nY) * 2 + r.k, r.c)
                count += 1
        elif group == b.next:
            pl.when(r.s < r.nS - 1)(lambda: tell(r.s + 1, r.c))
            pl.when(r.s > 0)(lambda: tell(r.s - 1, r.c))
        elif group == b.cross:
            for i in range(r.nC):
                c2 = lax.rem(r.c + i, r.nC)
                if i == 0:
                    pl.when(r.y != r.z)(lambda c2=c2: tell(r.z * 2 + r.k, c2))
                else:
                    tell(r.z * 2 + r.k, c2)
            for i in range(r.nY):
                for j in range(r.nX):
                    y2, x2 = lax.rem(r.y + i, r.nY), lax.rem(r.x + j, r.nX)
                    if i == 0 and j == 0:
                        pl.when(r.y != r.z)(lambda y2=y2, x2=x2: tell(y2 * 2 + r.k, r.y * r.nX + x2))
                    else:
                        tell(y2 * 2 + r.k, r.y * r.nX + x2)
            count += 2 * (r.nC - 1)
    if b.next in groups:
        last = r.nS - 1
        count = count + lax.div(last - r.s + last - 1, last) + lax.div(r.s + last - 1, last)
    if b.cross in groups:
        apart = (r.y - r.z) * (r.y - r.z)
        count = count + 2 * lax.div(apart + r.nY * r.nY - 1, r.nY * r.nY)
    pl.semaphore_wait(barrier, count)


def hidden_copy(r, i):
    slot = r.x * r.nY + r.y
    return rcopy(
        r.hidden,
        r.hg.at[slot],
        r.sems[b.hid_s].at[i],
        r.sems[b.hid_r].at[slot],
        r.z * 2 + r.k,
        lax.rem(r.c + i, r.nC),
    )


def pair_copy(r, src, dst, key):
    return rcopy(src, dst, r.sems[key + "_s"].at[0], r.sems[key + "_r"].at[0], r.y * 2 + 1 - r.k, r.c)


def line_copy(r, i, src, dst, key, slot):
    return rcopy(
        src, dst, r.sems[key + "_s"].at[i], r.sems[key + "_r"].at[slot], lax.rem(r.y + i, r.nY) * 2 + r.k, r.c
    )


def project(r):
    slot = r.x * r.nY + r.y
    half = r.nX // 2
    own_w = pltpu.make_async_copy(r.w_in, r.wp.at[pl.ds(r.k * half, half)], r.sems[b.loc].at[0])
    own_w.start()
    pair_copy(r, r.w_in, r.wp.at[pl.ds(r.k * half, half)], b.wp).start()
    for i in range(r.nC):
        if i == 0:
            pl.when(r.y != r.z)(lambda: hidden_copy(r, 0).start())
        else:
            hidden_copy(r, i).start()

    @pl.when(r.y == r.z)
    def _():
        r.hg[slot] = r.hidden[...]

    own_w.wait()
    pair_copy(r, r.w_in, r.wp.at[pl.ds((1 - r.k) * half, half)], b.wp).wait_recv()

    def arrive(slot2):
        rcopy(
            r.hidden, r.hg.at[slot2], r.sems[b.hid_s].at[0], r.sems[b.hid_r].at[slot2], r.z * 2 + r.k, r.c
        ).wait_recv()

    for i in range(1, r.nY + 1):
        y2 = lax.rem(r.y + i, r.nY)
        total = None
        for j in range(r.nX):
            x2 = lax.rem(r.x + j, r.nX)
            slot2 = x2 * r.nY + y2
            if i == r.nY and j == 0:
                pl.when(r.y != r.z)(lambda slot2=slot2: arrive(slot2))
            else:
                arrive(slot2)
            term = dot(r.hg[slot2], r.wp[x2])
            total = term if total is None else total + term
        if i < r.nY:
            r.xs[i - 1] = total.astype(BF16)
            line_copy(r, i, r.xs.at[i - 1], r.xr.at[r.y], b.xr, r.y).start()
        else:
            own = total
    for i in range(1, r.nY):
        y2 = lax.rem(r.y + i, r.nY)
        line_copy(r, i, r.xs.at[i - 1], r.xr.at[y2], b.xr, y2).wait_recv()
        own = own + r.xr[y2].astype(F32)
    x_rounded = own.astype(BF16)
    r.tail_s[...] = x_rounded[r.T - HALO :]

    def tail_copy(to):
        return rcopy(r.tail_s, r.tail_r, r.sems[b.tail_s].at[0], r.sems[b.tail_r].at[0], to, r.c)

    pl.when(r.s < r.nS - 1)(lambda: tail_copy(r.s + 1).start())
    r.xpad[pl.ds(HALO, r.T), :] = x_rounded.astype(F32)

    @pl.when(r.s == 0)
    def _():
        r.xpad[pl.ds(0, HALO), :] = jnp.zeros((HALO, r.C), F32)

    @pl.when(r.s > 0)
    def _():
        tail_copy(r.s - 1).wait_recv()
        r.xpad[pl.ds(0, HALO), :] = r.tail_r[...].astype(F32)

    conv = jnp.zeros((r.T, r.C), F32) + r.conv_b[...]
    for k in range(r.KC):
        conv = conv + r.conv_w[k : k + 1, :] * r.xpad[pl.ds(HALO - r.KC + 1 + k, r.T), :]
    r.conv_pre[...] = conv
    u = (conv * jax.nn.sigmoid(conv)).astype(BF16)
    r.u[...] = u
    r.part[:, :, pl.ds(0, r.R)] = contract_last(u, r.w_delta_in[...]).reshape(r.nC, r.RP, r.R)
    r.part[:, :, pl.ds(r.R, LANES)] = jnp.zeros((r.nC, r.RP, LANES), F32)
    r.part[:, :, pl.ds(r.R, 2 * r.N)] = contract_last(u, r.w_bc[...]).reshape(r.nC, r.RP, 2 * r.N)
    scatter_start(r, b.chan, r.part, r.part_r, b.p1)
    r.part_a[r.c] = scatter_sum(r, b.chan, r.part, r.part_r, b.p1)
    gather_start(r, b.chan, r.part_a, b.p2)
    recv_wait(r, b.chan, r.part_a, b.p2)
    full = r.part_a[...].reshape(r.T, r.R + LANES)
    r.low[...] = full[:, : r.R].astype(BF16)
    r.bcw[...] = full[:, r.R :]


def project_end(r):
    half = r.nX // 2
    for i in range(r.nC):
        if i == 0:
            pl.when(r.y != r.z)(lambda: hidden_copy(r, 0).wait_send())
        else:
            hidden_copy(r, i).wait_send()
    pair_copy(r, r.w_in, r.wp.at[pl.ds(r.k * half, half)], b.wp).wait_send()
    for i in range(1, r.nY):
        line_copy(r, i, r.xs.at[i - 1], r.xr.at[r.y], b.xr, r.y).wait_send()
    pl.when(r.s < r.nS - 1)(
        lambda: rcopy(
            r.tail_s, r.tail_r, r.sems[b.tail_s].at[0], r.sems[b.tail_r].at[0], r.s + 1, r.c
        ).wait_send()
    )
    send_wait(r, b.chan, r.part, b.p1)
    send_wait(r, b.chan, r.part_a, b.p2)


def wide(r, b):
    return jnp.concatenate([b] * (r.C // LANES), axis=1) if r.C > LANES else b


def block_mask(r, rows):
    row = lax.broadcasted_iota(jnp.int32, (rows, CH * r.N), 0)
    col = lax.broadcasted_iota(jnp.int32, (rows, CH * r.N), 1)
    return jnp.where(lax.rem(row, CH) == lax.div(col, r.N), 1.0, 0.0).astype(F32)


def pick(r):
    row = lax.broadcasted_iota(jnp.int32, (r.N, CH * r.N), 0)
    col = lax.broadcasted_iota(jnp.int32, (r.N, CH * r.N), 1)
    return jnp.where(lax.rem(col, r.N) == row, 1.0, 0.0).astype(F32)


def prepare(r):
    pre = dot(r.low[...], r.w_dt[...]) + r.dt_bias[...]
    r.pre[...] = pre
    delta = softplus(pre)
    r.delta[...] = delta
    u = r.u[...].astype(F32)
    r.du[...] = delta * u
    gate = r.gate_in[...].astype(F32)
    r.g[...] = r.out_grad[...].astype(F32) * (gate * jax.nn.sigmoid(gate))
    r.am[...] = -jnp.exp(r.a_log[...])
    turned = r.bcw[...].T
    for t in range(r.T):
        r.bx[t] = jnp.broadcast_to(turned[0 : r.N, t : t + 1], (r.N, LANES))
        r.cx[t] = jnp.broadcast_to(turned[r.N : 2 * r.N, t : t + 1], (r.N, LANES))
    r.sd[...] = jnp.sum(delta, 0, keepdims=True)


def forward(r, init, full):
    a_mat = r.am[...]
    if full:
        mask = block_mask(r, CH)
        r.hh[pl.ds(0, r.N), :] = init

    def chunk(j, h):
        base = pl.multiple_of(j * CH, CH)
        d = r.delta[pl.ds(base, CH), :]
        du = r.du[pl.ds(base, CH), :]
        kept = []
        for t in range(CH):
            at = pl.multiple_of((base + t) * r.N, r.N)
            a = jnp.exp(d[t : t + 1, :] * a_mat)
            r.aa[pl.ds(at, r.N), :] = a
            h = a * h + du[t : t + 1, :] * wide(r, r.bx[base + t])
            if full:
                r.hh[pl.ds(at + r.N, r.N), :] = h
                kept.append(h.astype(BF16))
        if full:
            rows = jnp.concatenate(kept, 0)
            r.y_scan[pl.ds(base, CH), :] = dot(r.cd[pl.ds(base, CH), :], rows)
            r.cm[pl.ds(base, CH), :] = mask * contract_last(r.g[pl.ds(base, CH), :].astype(BF16), rows)
        return h

    return lax.fori_loop(0, r.T // CH, chunk, init)


def backward(r, init, full):
    a_mat = r.am[...]
    mask = block_mask(r, CH)
    chunks = r.T // CH

    def chunk(i, carry):
        base = pl.multiple_of((chunks - 1 - i) * CH, CH)
        kap, acc = carry
        d = r.delta[pl.ds(base, CH), :]
        g = r.g[pl.ds(base, CH), :]
        lams, qas = [None] * CH, [None] * CH
        for t in reversed(range(CH)):
            at = pl.multiple_of((base + t) * r.N, r.N)
            lam = kap + wide(r, r.cx[base + t]) * g[t : t + 1, :]
            kap = r.aa[pl.ds(at, r.N), :] * lam
            if full:
                q = kap * r.hh[pl.ds(at, r.N), :]
                acc = acc + q * d[t : t + 1, :]
                qas[t] = (q * a_mat).astype(BF16)
                lams[t] = lam.astype(BF16)
        if full:
            lam_rows = jnp.concatenate(lams, 0)
            du = r.du[pl.ds(base, CH), :]
            r.s1[pl.ds(base, CH), :] = dot(r.bd[pl.ds(base, CH), :], lam_rows)
            r.s2[pl.ds(base, CH), :] = dot(mask.astype(BF16), jnp.concatenate(qas, 0))
            r.bm[pl.ds(base, CH), :] = mask * contract_last(du.astype(BF16), lam_rows)
        return kap, acc

    return lax.fori_loop(0, chunks, chunk, (init, jnp.zeros_like(init)))


def scan_free(r):
    zero = jnp.zeros((r.N, r.C), F32)
    r.ef[0] = forward(r, zero, False).astype(BF16)
    r.ef[1] = backward(r, zero, False)[0].astype(BF16)


def scan_exchange(r):
    r.st_r[r.s] = jnp.zeros((r.N, r.C), BF16)
    r.sd_r[r.s] = jnp.zeros((1, r.C), F32)
    copies = []
    for i, j, dev in peers(r, b.seq):
        copies.append(
            rcopy(
                r.ef.at[lax.div(r.s + i, r.nS)], r.st_r.at[r.s], r.sems[b.st_s].at[i], r.sems[b.st_r].at[r.s], *dev
            )
        )
        copies.append(rcopy(r.sd, r.sd_r.at[r.s], r.sems[b.sd_s].at[i], r.sems[b.sd_r].at[r.s], *dev))
    for copy in copies:
        copy.start()
    recv_wait(r, b.seq, r.sd_r, b.sd)
    recv_wait(r, b.seq, r.st_r, b.st)
    a_mat = r.am[...]
    state = jnp.zeros((r.N, r.C), F32)
    for j in range(r.nS - 1):
        new = jnp.exp(a_mat * r.sd_r[j]) * state + r.st_r[j].astype(F32)
        state = jnp.where(j < r.s, new, state)
    r.h_in[...] = state
    adj = jnp.zeros((r.N, r.C), F32)
    for j in range(r.nS - 1, 0, -1):
        new = jnp.exp(a_mat * r.sd_r[j]) * adj + r.st_r[j].astype(F32)
        adj = jnp.where(j > r.s, new, adj)
    r.l_in[...] = adj
    for copy in copies:
        copy.wait_send()


def scan_full(r):
    picked = pick(r)
    tall = block_mask(r, r.T)
    r.bd[...] = (tall * dot(r.bcw[:, pl.ds(0, r.N)], picked)).astype(BF16)
    r.cd[...] = (tall * dot(r.bcw[:, pl.ds(r.N, r.N)], picked)).astype(BF16)
    forward(r, r.h_in[...], True)
    a_adj = backward(r, r.l_in[...], True)[1]
    r.alog_p[...] = a_adj * r.am[...]
    s1 = r.s1[...]
    u = r.u[...].astype(F32)
    skip = r.skip_d[...]
    pre_adj = ((u * s1 + r.s2[...]) * jax.nn.sigmoid(r.pre[...])).astype(BF16)
    r.uu[...] = r.delta[...] * s1 + skip * r.g[...]
    exact = lax.Precision.HIGHEST
    nt = (((1,), (1,)), ((), ()))
    b_adj = lax.dot_general(r.bm[...], picked, nt, precision=exact, preferred_element_type=F32)
    c_adj = lax.dot_general(r.cm[...], picked, nt, precision=exact, preferred_element_type=F32)
    r.part2[:, :, pl.ds(0, r.R)] = contract_last(pre_adj, r.w_dt[...]).reshape(r.nC, r.RP, r.R)
    r.part2[:, :, pl.ds(r.R, LANES)] = jnp.zeros((r.nC, r.RP, LANES), F32)
    r.part2[:, :, pl.ds(r.R, r.N)] = b_adj.reshape(r.nC, r.RP, r.N)
    r.part2[:, :, pl.ds(r.R + r.N, r.N)] = c_adj.reshape(r.nC, r.RP, r.N)
    r.dt_p[...] = contract_first(r.low[...], pre_adj).astype(BF16).reshape(r.nS, r.R // r.nS, r.C)
    gate = r.gate_in[...].astype(F32)
    y_out = r.y_scan[...] + skip * u
    r.gate_grad[...] = (r.out_grad[...].astype(F32) * y_out * silu_slope(gate)).astype(BF16)


def grad_copy(r, i, j):
    y2, x2 = lax.rem(r.y + i, r.nY), lax.rem(r.x + j, r.nX)
    n = i * r.nX + j
    return rcopy(
        r.hs.at[n], r.hr.at[r.c], r.sems[b.hg_s].at[n], r.sems[b.hg_r].at[r.c], y2 * 2 + r.k, r.y * r.nX + x2
    )


def gradients(r):
    scale = 1.0 / math.sqrt(r.T * r.nS)
    half = r.nX // 2
    nb, na = 2 * r.N // r.nS, r.N // r.nS
    scatter_start(r, b.chan, r.part2, r.part2_r, b.p3)
    scatter_start(r, b.seq, r.dt_p, r.dt_r, b.d1)
    r.part2_a[r.c] = scatter_sum(r, b.chan, r.part2, r.part2_r, b.p3)
    gather_start(r, b.chan, r.part2_a, b.p4)
    r.dt_a[r.s] = scatter_sum(r, b.seq, r.dt_p, r.dt_r, b.d1).astype(BF16)
    gather_start(r, b.seq, r.dt_a, b.d2)
    recv_wait(r, b.chan, r.part2_a, b.p4)
    full = r.part2_a[...].reshape(r.T, r.R + LANES)
    low_adj = full[:, : r.R].astype(BF16)
    bc_adj = full[:, r.R : r.R + 2 * r.N].astype(BF16)
    u_adj = r.uu[...] + dot(low_adj, r.w_delta_in[...]) + dot(bc_adj, r.w_bc[...])
    conv_adj = u_adj * silu_slope(r.conv_pre[...])
    r.cpad[pl.ds(0, r.T), :] = conv_adj

    def head_copy(to):
        return rcopy(
            r.cpad.at[pl.ds(0, HEAD)],
            r.cpad.at[pl.ds(r.T, HEAD)],
            r.sems[b.head_s].at[0],
            r.sems[b.head_r].at[0],
            to,
            r.c,
        )

    pl.when(r.s > 0)(lambda: head_copy(r.s - 1).start())

    @pl.when(r.s == r.nS - 1)
    def _():
        r.cpad[pl.ds(r.T, HEAD), :] = jnp.zeros((HEAD, r.C), F32)

    u = r.u[...]
    r.di_p[...] = contract_first(low_adj, u).astype(BF16).reshape(r.nS, r.R // r.nS, r.C)
    bc_term = contract_first(bc_adj, u)
    alog = r.alog_p[...]
    r.mi_p[...] = jnp.zeros_like(r.mi_p)
    for j in range(r.nS):
        r.mi_p[j, pl.ds(0, nb), :] = bc_term[j * nb : (j + 1) * nb]
        r.mi_p[j, pl.ds(nb, na), :] = alog[j * na : (j + 1) * na]

    pl.when(r.s < r.nS - 1)(lambda: head_copy(r.s + 1).wait_recv())
    x_adj = jnp.zeros((r.T, r.C), F32)
    for k in range(r.KC):
        x_adj = x_adj + r.conv_w[k : k + 1, :] * r.cpad[pl.ds(r.KC - 1 - k, r.T), :]
    r.xg[r.y] = x_adj.astype(BF16)
    for i in range(1, r.nY):
        line_copy(r, i, r.xg.at[r.y], r.xg.at[r.y], b.xg, r.y).start()
    scatter_start(r, b.seq, r.di_p, r.di_r, b.d3)
    scatter_start(r, b.seq, r.mi_p, r.mi_r, b.d5)

    for i in range(r.nY):
        y2 = lax.rem(r.y + i, r.nY)
        if i:
            line_copy(r, i, r.xg.at[y2], r.xg.at[y2], b.xg, y2).wait_recv()
        for j in range(r.nX):
            x2 = lax.rem(r.x + j, r.nX)
            n = i * r.nX + j
            r.hs[n] = contract_last(r.xg[y2], r.wp[x2]).astype(BF16)
            if n == 0:

                @pl.when(r.y == r.z)
                def _():
                    r.hr[r.c] = r.hs[0]

                pl.when(r.y != r.z)(lambda: grad_copy(r, 0, 0).start())
            else:
                grad_copy(r, i, j).start()

    x_all = r.xg[...].reshape(r.nY * r.T, r.C)

    def weight(x2):
        rows = r.hg[pl.ds(x2 * r.nY, r.nY)].reshape(r.nY * r.T, r.DH)
        return contract_first(rows, x_all)

    for j in range(half):
        r.ws[j] = weight((1 - r.k) * half + j).astype(BF16)
    pair_copy(r, r.ws, r.wr, b.wg).start()
    r.di_a[r.s] = scatter_sum(r, b.seq, r.di_p, r.di_r, b.d3).astype(BF16)
    gather_start(r, b.seq, r.di_a, b.d4)
    r.mi_a[r.s] = scatter_sum(r, b.seq, r.mi_p, r.mi_r, b.d5)
    gather_start(r, b.seq, r.mi_a, b.d6)
    for j in range(half):
        r.w_in_grad[j] = weight(r.k * half + j)
    pair_copy(r, r.ws, r.wr, b.wg).wait_recv()
    for j in range(half):
        r.w_in_grad[j] = (r.w_in_grad[j] + r.wr[j].astype(F32)) * scale

    recv_wait(r, b.seq, r.dt_a, b.d2)
    r.w_dt_grad[...] = r.dt_a[...].astype(F32).reshape(r.R, r.C) * scale
    total = None
    for j in range(r.nC):
        c2 = lax.rem(r.c + j, r.nC)
        wait = rcopy(
            r.hs.at[0], r.hr.at[c2], r.sems[b.hg_s].at[0], r.sems[b.hg_r].at[c2], r.z * 2 + r.k, c2
        )
        if j == 0:
            pl.when(r.y != r.z)(lambda wait=wait: wait.wait_recv())
        else:
            wait.wait_recv()
        term = r.hr[c2].astype(F32)
        total = term if total is None else total + term
    r.hidden_grad[...] = total.astype(BF16)
    recv_wait(r, b.seq, r.di_a, b.d4)
    r.w_delta_in_grad[...] = r.di_a[...].astype(F32).reshape(r.R, r.C) * scale
    recv_wait(r, b.seq, r.mi_a, b.d6)
    for j in range(r.nS):
        r.w_bc_grad[pl.ds(j * nb, nb), :] = r.mi_a[j, pl.ds(0, nb), :] * scale
        r.a_log_grad[pl.ds(j * na, na), :] = r.mi_a[j, pl.ds(nb, na), :] * scale

    send_wait(r, b.chan, r.part2, b.p3)
    send_wait(r, b.chan, r.part2_a, b.p4)
    for name, key in ((b.dt_p, b.d1), (b.dt_a, b.d2), (b.di_p, b.d3), (b.di_a, b.d4), (b.mi_p, b.d5), (b.mi_a, b.d6)):
        send_wait(r, b.seq, getattr(r, name), key)
    pl.when(r.s > 0)(lambda: head_copy(r.s - 1).wait_send())
    for i in range(1, r.nY):
        line_copy(r, i, r.xg.at[r.y], r.xg.at[r.y], b.xg, r.y).wait_send()
    for i in range(r.nY):
        for j in range(r.nX):
            if i == 0 and j == 0:
                pl.when(r.y != r.z)(lambda: grad_copy(r, 0, 0).wait_send())
            else:
                grad_copy(r, i, j).wait_send()
    pair_copy(r, r.ws, r.wr, b.wg).wait_send()


def tables(dim):
    d = types.SimpleNamespace(**dim)
    t, c, n, rows, q = d.T, d.C, d.N, d.R, d.R // d.nS
    small = -(-(3 * n // d.nS) // 8) * 8
    wide_row = rows + LANES
    buffers = dict(
        hg=((d.nC, t, d.DH), BF16),
        wp=((d.nX, d.DH, c), BF16),
        xs=((d.nY - 1, t, c), BF16),
        xr=((d.nY, t, c), BF16),
        tail_s=((HALO, c), BF16),
        tail_r=((HALO, c), BF16),
        xpad=((HALO + t, c), F32),
        conv_pre=((t, c), F32),
        u=((t, c), BF16),
        part=((d.nC, d.RP, wide_row), F32),
        part_r=((d.nC, d.RP, wide_row), F32),
        part_a=((d.nC, d.RP, wide_row), F32),
        low=((t, rows), BF16),
        bcw=((t, LANES), F32),
        pre=((t, c), F32),
        delta=((t, c), F32),
        du=((t, c), F32),
        g=((t, c), F32),
        am=((n, c), F32),
        bx=((t, n, LANES), F32),
        cx=((t, n, LANES), F32),
        sd=((1, c), F32),
        aa=((t * n, c), F32),
        hh=(((t + 1) * n, c), F32),
        ef=((2, n, c), BF16),
        st_r=((d.nS, n, c), BF16),
        sd_r=((d.nS, 1, c), F32),
        h_in=((n, c), F32),
        l_in=((n, c), F32),
        bd=((t, CH * n), BF16),
        cd=((t, CH * n), BF16),
        bm=((t, CH * n), F32),
        cm=((t, CH * n), F32),
        y_scan=((t, c), F32),
        s1=((t, c), F32),
        s2=((t, c), F32),
        uu=((t, c), F32),
        alog_p=((n, c), F32),
        part2=((d.nC, d.RP, wide_row), F32),
        part2_r=((d.nC, d.RP, wide_row), F32),
        part2_a=((d.nC, d.RP, wide_row), F32),
        dt_p=((d.nS, q, c), BF16),
        dt_r=((d.nS, q, c), BF16),
        dt_a=((d.nS, q, c), BF16),
        di_p=((d.nS, q, c), BF16),
        di_r=((d.nS, q, c), BF16),
        di_a=((d.nS, q, c), BF16),
        mi_p=((d.nS, small, c), F32),
        mi_r=((d.nS, small, c), F32),
        mi_a=((d.nS, small, c), F32),
        cpad=((t + HEAD, c), F32),
        xg=((d.nY, t, c), BF16),
        hs=((d.nC, t, d.DH), BF16),
        hr=((d.nC, t, d.DH), BF16),
        ws=((d.nX // 2, d.DH, c), BF16),
        wr=((d.nX // 2, d.DH, c), BF16),
        hidden_grad=((t, d.DH), BF16),
        gate_grad=((t, c), BF16),
        w_in_grad=((d.nX // 2, d.DH, c), F32),
        w_delta_in_grad=((rows, c), F32),
        w_bc_grad=((2 * n, c), F32),
        w_dt_grad=((rows, c), F32),
        a_log_grad=((n, c), F32),
    )
    sems = dict(
        loc=1,
        hid_s=d.nC,
        hid_r=d.nC,
        wp_s=1,
        wp_r=1,
        xr_s=d.nY,
        xr_r=d.nY,
        tail_s=1,
        tail_r=1,
        head_s=1,
        head_r=1,
        xg_s=d.nY,
        xg_r=d.nY,
        hg_s=d.nC,
        hg_r=d.nC,
        wg_s=1,
        wg_r=1,
    )
    for key, count in ((b.p1, d.nC), (b.p2, d.nC), (b.p3, d.nC), (b.p4, d.nC), (b.st, d.nS), (b.sd, d.nS)):
        sems[key + "_s"] = sems[key + "_r"] = count
    for key in (b.d1, b.d2, b.d3, b.d4, b.d5, b.d6):
        sems[key + "_s"] = sems[key + "_r"] = d.nS
    return buffers, sems


def run(dim, phases, groups, values, ins, outs, scratch, sem_names, number, cost):
    buffers, sem_sizes = tables(dim)

    def body(*refs):
        r = types.SimpleNamespace(**dim)
        for name, ref in zip(ins + outs + scratch, refs):
            setattr(r, name, ref)
        r.sems = dict(zip(sem_names, refs[len(ins) + len(outs) + len(scratch) :]))
        if groups:
            r.s, r.c = lax.axis_index(b.seq), lax.axis_index(b.chan)
            r.y, r.k = lax.div(r.s, 2), lax.rem(r.s, 2)
            r.z, r.x = lax.div(r.c, r.nX), lax.rem(r.c, r.nX)
            greet(r, groups)
        for phase in phases:
            phase(r)

    space = pl.BlockSpec(memory_space=pltpu.VMEM)
    extra = dict(collective_id=number, has_side_effects=True) if groups else {}
    results = pl.pallas_call(
        body,
        out_shape=[jax.ShapeDtypeStruct(*buffers[name]) for name in outs],
        in_specs=[space] * len(ins),
        out_specs=[space] * len(outs),
        scratch_shapes=[pltpu.VMEM(*buffers[name]) for name in scratch]
        + [pltpu.SemaphoreType.DMA((sem_sizes[name],)) for name in sem_names],
        compiler_params=pltpu.CompilerParams(vmem_limit_bytes=56 << 20, **extra),
        cost_estimate=pl.CostEstimate(flops=cost, bytes_accessed=4 << 20, transcendentals=0),
        name=phases[0].__name__,
    )(*[values[name] for name in ins])
    values.update(zip(outs, results))


ORDER = [b.hidden_grad, b.gate_grad, b.w_in_grad, b.w_delta_in_grad, b.w_bc_grad, b.w_dt_grad, b.a_log_grad]


def keys(*names):
    return [name + end for name in names for end in ("_s", "_r")]


def per_device(
    seq, chan, hidden, gate_in, out_grad, w_in, conv_w, conv_b, w_delta_in, w_bc, w_dt, dt_bias, a_log, skip_d
):
    lines = seq // 2
    dim = dict(
        nS=seq,
        nC=chan,
        nY=lines,
        nX=chan // lines,
        T=hidden.shape[0],
        DH=hidden.shape[1],
        C=w_in.shape[1],
        R=w_delta_in.shape[0],
        N=a_log.shape[0],
        KC=conv_w.shape[0],
        RP=hidden.shape[0] // chan,
    )
    v = dict(
        hidden=hidden,
        gate_in=gate_in,
        out_grad=out_grad,
        w_in=w_in.reshape(dim[b.nX] // 2, dim[b.DH], dim[b.C]),
        conv_w=conv_w,
        conv_b=conv_b[None],
        w_delta_in=w_delta_in,
        w_bc=w_bc,
        w_dt=w_dt,
        dt_bias=dt_bias[None],
        a_log=a_log,
        skip_d=skip_d[None],
    )
    go = functools.partial(run, dim)
    go(
        [project, project_end],
        [b.cross, b.pair, b.line, b.next, b.chan],
        v,
        [b.hidden, b.w_in, b.conv_w, b.conv_b, b.w_delta_in, b.w_bc],
        [b.hg, b.wp, b.conv_pre, b.u, b.low, b.bcw],
        [b.xs, b.xr, b.tail_s, b.tail_r, b.xpad, b.part, b.part_r, b.part_a],
        [b.loc] + keys(b.hid, b.wp, b.xr, b.tail, b.p1, b.p2),
        0,
        600_000_000,
    )
    go(
        [prepare, scan_free],
        [],
        v,
        [b.low, b.u, b.bcw, b.w_dt, b.dt_bias, b.a_log, b.gate_in, b.out_grad],
        [b.pre, b.delta, b.du, b.g, b.am, b.bx, b.cx, b.sd, b.ef],
        [b.aa],
        [],
        0,
        50_000_000,
    )
    go([scan_exchange], [b.seq], v, [b.ef, b.sd, b.am], [b.h_in, b.l_in], [b.st_r, b.sd_r], keys(b.st, b.sd), 1, 1_000_000)
    go(
        [scan_full],
        [],
        v,
        [b.low, b.u, b.bcw, b.w_dt, b.gate_in, b.out_grad, b.skip_d]
        + [b.pre, b.delta, b.du, b.g, b.am, b.bx, b.cx, b.h_in, b.l_in],
        [b.gate_grad, b.uu, b.alog_p, b.part2, b.dt_p],
        [b.aa, b.hh, b.bd, b.cd, b.bm, b.cm, b.y_scan, b.s1, b.s2],
        [],
        0,
        100_000_000,
    )
    go(
        [gradients],
        [b.cross, b.pair, b.line, b.next, b.chan, b.seq],
        v,
        [b.hg, b.wp, b.conv_pre, b.u, b.conv_w, b.w_delta_in, b.w_bc, b.uu, b.alog_p, b.part2, b.dt_p],
        [name for name in ORDER if name != b.gate_grad],
        [b.part2_r, b.part2_a, b.dt_r, b.dt_a, b.di_p, b.di_r, b.di_a, b.mi_p, b.mi_r, b.mi_a]
        + [b.cpad, b.xg, b.hs, b.hr, b.ws, b.wr],
        keys(b.head, b.xg, b.hg, b.wg, b.p3, b.p4, b.d1, b.d2, b.d3, b.d4, b.d5, b.d6),
        2,
        1_200_000_000,
    )
    v[b.w_in_grad] = v[b.w_in_grad].reshape(w_in.shape)
    return tuple(v[name] for name in ORDER)


def solution(mesh):
    placed = (
        P(b.seq, b.chan),
        P(b.seq, b.chan),
        P(b.seq, b.chan),
        P(b.seq, b.chan),
        P(None, b.chan),
        P(b.chan),
        P(None, b.chan),
        P(None, b.chan),
        P(None, b.chan),
        P(b.chan),
        P(None, b.chan),
        P(b.chan),
    )
    return jax.shard_map(
        functools.partial(per_device, mesh.shape[b.seq], mesh.shape[b.chan]),
        mesh=mesh,
        in_specs=placed,
        out_specs=(
            P(b.seq, b.chan),
            P(b.seq, b.chan),
            P(b.seq, b.chan),
            P(None, b.chan),
            P(None, b.chan),
            P(None, b.chan),
            P(None, b.chan),
        ),
        check_vma=False,
    )
```

time: 803 us -> 174 us (0.22); the launches traced: 794 us -> 174 us
  waiting for transfers between devices: 346 us -> 0 us
  other arithmetic: 178 us -> 0 us
  Pallas kernels: 0 us -> 166 us
  blocking collectives: 129 us -> 0 us
  local copies, waits for them, and re-layouts: 84.2 us -> 6.7 us
  matrix products: 19.2 us -> 0 us
  loops' own time: 16.1 us -> 0 us
  between operations: 14.7 us -> 0.66 us
    pallas_call x0 -> x5, Pallas kernels: none -> 166 us  [run(): pl.pallas_call(body, out_shape=[jax.ShapeDtypeStruct(*buffers[name]) for...]
    psum x3 -> x0, waiting for transfers between devices: 151 us -> none  [the longest x1 79.9 us: per_device(): lax.psum(low_part.astype(jnp.bfloat16), 'chan').astype(jnp.float32)]
    reduce_sum x240 -> x0, other arithmetic: 128 us -> none  [the longest x128 44.6 us: token_step(): (d_row * u_row)[None, :] * b_row[:, None]]
    reduce_scatter x2 -> x0, waiting for transfers between devices: 111 us -> none  [the longest x1 75 us: per_device(): lax.psum_scatter(partial_in.astype(jnp.bfloat16), 'chan', scatter_dimensi...]
    psum x3 -> x0, blocking collectives: 88.3 us -> none  [the longest x1 33.9 us: per_device(): lax.psum(contract_last(u_rounded, w_bc).astype(jnp.bfloat16), 'chan')]
    all_gather x2 -> x0, waiting for transfers between devices: 80.6 us -> none  [the longest x1 45.7 us: per_device(): whole = lax.all_gather(hidden, 'chan', axis=1, tiled=True)]
    dynamic_update_slice x284 -> x0, local copies, waits for them, and re-layouts: 56.7 us -> none  [the longest x272 52.6 us: step(): return lax.scan(token_step, carried, pieces, unroll=8)]
    all_gather x3 -> x0, blocking collectives: 40.6 us -> none  [the longest x2 27.9 us: entering(): lax.all_gather(a.astype(kind), axis)]
  transfers between devices with their start and end apart: 9 -> 0, of which waited for: 9 -> 0; matrix products, arithmetic and copies ran while one was open for 2% -> 0% of each run, Pallas kernels for 0% -> 0%
where the time goes in v1:
time: 174 us
  Pallas kernels  166 us (95%)
  local copies, waits for them, and re-layouts  6.7 us (4%)
    pallas_call x5, Pallas kernels, run(): pl.pallas_call(body, out_shape=[jax.ShapeDtypeStruct(*buffers[name]) for...  166 us
    unnamed x14, local copies, waits for them, and re-layouts  6.7 us

profile of v1, /device:TPU:1, one launch (start us, length us, event | category | flops | bytes accessed | tf_op | source)
XLA Modules:
  0.0 173.7 jit_solution(9847916666359358407)
XLA Ops:
  0.6 88.1 %project.1 = (bf16[16,128,256]{2,1,0:T(8,128)(2,1)}, bf16[4,256,512]{2,1,0:T(8,128)(2,1)}, f32[128,512]{1,0:T(8,128)}, bf16[128,512]{1,0:T(8,128)(2,1)}, bf16[128,256]{1,0:T(8,128)(2,1)}, /*index=5*/f32[128,128]{1,0:T(8,128)}) custom-call(bf16[128,256]{1,0:T(8,128)(2,1)} %refs_0_.1, bf16[2,256,512]{2,1,0:T(8,128)(2,1)} %bitcast.8, f32[4,512]{1,0:T(4,128)} %refs_4_.5, ...), custom_call_target="tpu_custom_call" | custom-call | flops 600000000 | bytes 4194304 | tf_op jit(solution)/shard_map/project/pallas_call | solution.py:677
  88.8 5.5 %prepare.1 = (f32[128,512]{1,0:T(8,128)}, f32[128,512]{1,0:T(8,128)}, f32[128,512]{1,0:T(8,128)}, f32[128,512]{1,0:T(8,128)}, f32[16,512]{1,0:T(8,128)}, /*index...) custom-call(bf16[128,256]{1,0:T(8,128)(2,1)} %get-tuple-element.39.refs_0_, ...), custom_call_target="tpu_custom_call" | custom-call | flops 50000000 | bytes 4194304 | tf_op jit(solution)/shard_map/prepare/pallas_call | solution.py:677
  94.3 12.0 %scan_exchange.1 = (f32[16,512]{1,0:T(8,128)}, f32[16,512]{1,0:T(8,128)}) custom-call(bf16[2,16,512]{2,1,0:T(8,128)(2,1)} %get-tuple-element.48.refs_0_, f32[1,512]{1,0:T(1,128)} %get-tuple-element.49.refs_1_, f32[16,512]{1,0:T(8,128)} %get-tuple-element.45.refs_2_.refs_11_), custom_call_target="tpu_custom_call" | custom-call | flops 1000000 | bytes 4194304 | tf_op jit(solution)/shard_map/scan_exchange/pallas_call | solution.py:677
  106.3 9.4 %scan_full.1 = (bf16[128,512]{1,0:T(8,128)(2,1)}, f32[128,512]{1,0:T(8,128)}, f32[16,512]{1,0:T(8,128)}, f32[16,8,384]{2,1,0:T(8,128)}, bf16[8,32,512]{2,1,0:T(8,128)(2,1)}) custom-call(bf16[128,256]{1,0:T(8,128)(2,1)} %get-tuple-element.39.refs_0_, bf16[128,512]{1,0:T(8,128)(2,1)} %get-tuple-element.38.refs_1_.refs_3_, ...), custom_call_target="tpu_custom_call" | custom-call | flops 100000000 | bytes 4194304 | tf_op jit(solution)/shard_map/scan_full/pallas_call | solution.py:677
  115.7 51.3 %gradients.1 = (bf16[128,256]{1,0:T(8,128)(2,1)}, f32[2,256,512]{2,1,0:T(8,128)}, f32[256,512]{1,0:T(8,128)}, f32[32,512]{1,0:T(8,128)}, f32[256,512]{1,0:T(8,128)}, /*index=5*/f32[16,512]{1,0:T(8,128)}) custom-call(bf16[16,128,256]{2,1,0:T(8,128)(2,1)} %get-tuple-element.35.refs_0_, bf16[4,256,512]{2,1,0:T(8,128)(2,1)} %get-tuple-element.36.refs_1_, ...), custom_call_target="tpu_custom_call" | custom-call | flops 1200000000 | bytes 4194304 | tf_op jit(solution)/shard_map/gradients/pallas_call | solution.py:677
  167.0 1.5 copy.25
  168.5 0.0 copy-start.1
  168.5 2.3 %copy.26 = f32[512,512]{1,0:T(8,128)} copy(f32[512,512]{1,0:T(8,128)} %bitcast.5) | data formatting | bytes 2097152
  170.8 0.0 copy-done.1
  170.8 0.0 copy-start.2
  170.8 0.0 copy-start
  170.8 0.8 copy.27
  171.6 0.1 copy-done.2
  171.7 0.6 copy.28
  172.3 0.0 copy-done
  172.3 0.0 copy-start.3
  172.3 0.8 copy.29
  173.1 0.0 copy-done.3
  173.1 0.6 copy.30
Async XLA Ops:
  168.5 2.3 %copy-start.1 = (f32[256,512]{1,0:T(8,128)S(1)}, f32[256,512]{1,0:T(8,128)}, u32[]{:S(2)}) copy-start(f32[256,512]{1,0:T(8,128)} %get-tuple-element.73) | copy-start | bytes 1572868
  170.8 0.9 copy-start.2
  170.8 1.5 copy-start
  172.3 0.8 copy-start.3

commit v2 on v1

v2 whole, which is shorter than its diff:
```python
import functools
import math
import types

import jax
import jax.numpy as jnp
from jax import lax
from jax.experimental import pallas as pl
from jax.experimental.pallas import tpu as pltpu
from jax.sharding import PartitionSpec as P

MESH = pl.DeviceIdType.MESH


class Names:
    def __getattr__(self, name):
        return name


b = Names()
F32, BF16 = jnp.float32, jnp.bfloat16
CH = 16
LANES = 128
HALO = 16
HEAD = 8


def contract_last(left, right):
    return lax.dot_general(left, right, (((1,), (1,)), ((), ())), preferred_element_type=F32)


def contract_first(left, right):
    return lax.dot_general(left, right, (((0,), (0,)), ((), ())), preferred_element_type=F32)


def dot(left, right):
    return jnp.dot(left, right, preferred_element_type=F32)


def silu_slope(values):
    sig = jax.nn.sigmoid(values)
    return sig * (1.0 + values * (1.0 - sig))


def softplus(v):
    return jnp.maximum(v, 0.0) + jnp.log1p(jnp.exp(-jnp.abs(v)))


def rcopy(src, dst, send, recv, seq, chan):
    return pltpu.make_async_remote_copy(
        src_ref=src,
        dst_ref=dst,
        send_sem=send,
        recv_sem=recv,
        device_id=dict(seq=seq, chan=chan),
        device_id_type=MESH,
    )


def ring(r, group):
    if group == b.seq:
        return r.s, r.nS, lambda j: (j, r.c)
    return r.c, r.nC, lambda j: (r.s, j)


def peers(r, group):
    me, n, dev = ring(r, group)
    for i in range(1, n):
        j = lax.rem(me + i, n)
        yield i, j, dev(j)


def start(r, copy, when=None):
    r.sent.append((copy, when))
    if when is None:
        copy.start()
    else:
        pl.when(when)(copy.start)


def flush(r):
    for copy, when in r.sent:
        if when is None:
            copy.wait_send()
        else:
            pl.when(when)(copy.wait_send)
    r.sent.clear()


def scatter_start(r, group, src, dst, key):
    me = ring(r, group)[0]
    for i, j, dev in peers(r, group):
        start(r, rcopy(src.at[j], dst.at[me], r.sems[key + "_s"].at[i], r.sems[key + "_r"].at[me], *dev))


def gather_start(r, group, buf, key):
    me = ring(r, group)[0]
    for i, j, dev in peers(r, group):
        start(r, rcopy(buf.at[me], buf.at[me], r.sems[key + "_s"].at[i], r.sems[key + "_r"].at[me], *dev))


def recv_wait(r, group, buf, key):
    for i, j, dev in peers(r, group):
        rcopy(buf.at[j], buf.at[j], r.sems[key + "_s"].at[i], r.sems[key + "_r"].at[j], *dev).wait_recv()


def scatter_sum(r, group, src, dst, key):
    me = ring(r, group)[0]
    total = src[me].astype(F32)
    recv_wait(r, group, dst, key)
    for i, j, dev in peers(r, group):
        total = total + dst[j].astype(F32)
    return total


def pair_copy(r, src, dst, key):
    return rcopy(src, dst, r.sems[key + "_s"].at[0], r.sems[key + "_r"].at[0], r.y * 2 + 1 - r.k, r.c)


def line_copy(r, i, src, dst, key, slot, part=0):
    at = part * r.nY
    return rcopy(
        src,
        dst,
        r.sems[key + "_s"].at[at + i],
        r.sems[key + "_r"].at[at + slot],
        lax.rem(r.y + i, r.nY) * 2 + r.k,
        r.c,
    )


def plane_copy(r, i, along_x, src, dst, key, slot):
    at, seq = (0 if along_x else r.nX), r.s
    chan = r.z * r.nX + lax.rem(r.x + i, r.nX) if along_x else lax.rem(r.z + i, r.nY) * r.nX + r.x
    return rcopy(src, dst, r.sems[key + "_s"].at[at + i], r.sems[key + "_r"].at[at + slot], seq, chan)


def greet(r, groups):
    barrier = pltpu.get_barrier_semaphore()
    count = 0

    def tell(seq, chan):
        pl.semaphore_signal(barrier, inc=1, device_id=dict(seq=seq, chan=chan), device_id_type=MESH)

    for group in groups:
        if group in (b.seq, b.chan):
            for i, j, dev in peers(r, group):
                tell(*dev)
                count += 1
        elif group == b.cross:
            for i in range(r.nC):
                c2 = lax.rem(r.c + i, r.nC)
                if i == 0:
                    pl.when(r.y != r.z)(lambda c2=c2: tell(r.z * 2 + r.k, c2))
                else:
                    tell(r.z * 2 + r.k, c2)
            for i in range(r.nY):
                for j in range(r.nX):
                    y2, x2 = lax.rem(r.y + i, r.nY), lax.rem(r.x + j, r.nX)
                    if i == 0 and j == 0:
                        pl.when(r.y != r.z)(lambda y2=y2, x2=x2: tell(y2 * 2 + r.k, r.y * r.nX + x2))
                    else:
                        tell(y2 * 2 + r.k, r.y * r.nX + x2)
            count += 2 * (r.nC - 1)
    if b.cross in groups:
        apart = (r.y - r.z) * (r.y - r.z)
        count = count + 2 * lax.div(apart + r.nY * r.nY - 1, r.nY * r.nY)
    pl.semaphore_wait(barrier, count)


def take_hidden(r):
    half, cut = r.nX // 2, r.T // 2
    own_w = pltpu.make_async_copy(r.w_in, r.wp.at[pl.ds(r.k * half, half)], r.sems[b.loc].at[0])
    own_w.start()
    turn = rcopy(
        r.hidden, r.hg.at[r.x, r.y], r.sems[b.tu_s].at[0], r.sems[b.tu_r].at[0], r.z * 2 + r.k, r.y * r.nX + r.x
    )
    start(r, turn, r.y != r.z)
    start(r, pair_copy(r, r.w_in, r.wp.at[pl.ds(r.k * half, half)], b.wp))

    @pl.when(r.y == r.z)
    def _():
        r.hg[r.x, r.y] = r.hidden[...]

    gate = r.gate_in[...].astype(F32)
    sig = jax.nn.sigmoid(gate)
    grad = r.out_grad[...].astype(F32)
    r.g[...] = grad * (gate * sig)
    r.gs[...] = grad * (sig * (1.0 + gate * (1.0 - sig)))
    r.am[...] = -jnp.exp(r.a_log[...])
    r.part[:, :, pl.ds(r.R, LANES)] = jnp.zeros((r.nC, r.RP, LANES), F32)
    r.part2[:, :, pl.ds(r.R, LANES)] = jnp.zeros((r.nC, r.RP, LANES), F32)
    own_w.wait()

    @pl.when(r.y != r.z)
    def _():
        rcopy(
            r.hidden, r.hg.at[r.x, r.z], r.sems[b.tu_s].at[0], r.sems[b.tu_r].at[0], r.z * 2 + r.k, r.y * r.nX + r.x
        ).wait_recv()

    low, high = pl.ds(0, cut), pl.ds(cut, r.T - cut)
    for i in range(1, r.nX):
        start(r, plane_copy(r, i, True, r.hg.at[r.x, r.z, low], r.hg.at[r.x, r.z, low], b.g1, r.x))
        start(r, plane_copy(r, i, False, r.hg.at[r.x, r.z, high], r.hg.at[r.x, r.z, high], b.g1, r.z))
    for i in range(1, r.nX):
        x2, z2 = lax.rem(r.x + i, r.nX), lax.rem(r.z + i, r.nY)
        plane_copy(r, i, True, r.hg.at[x2, r.z, low], r.hg.at[x2, r.z, low], b.g1, x2).wait_recv()
        plane_copy(r, i, False, r.hg.at[r.x, z2, high], r.hg.at[r.x, z2, high], b.g1, z2).wait_recv()
    for i in range(1, r.nX):
        start(r, plane_copy(r, i, False, r.hg.at[:, r.z, low], r.hg.at[:, r.z, low], b.g2, r.z))
        start(r, plane_copy(r, i, True, r.hg.at[r.x, :, high], r.hg.at[r.x, :, high], b.g2, r.x))
    pair_copy(r, r.w_in, r.wp.at[pl.ds((1 - r.k) * half, half)], b.wp).wait_recv()
    for i in range(1, r.nX):
        x2, z2 = lax.rem(r.x + i, r.nX), lax.rem(r.z + i, r.nY)
        plane_copy(r, i, True, r.hg.at[x2, :, high], r.hg.at[x2, :, high], b.g2, x2).wait_recv()
        plane_copy(r, i, False, r.hg.at[:, z2, low], r.hg.at[:, z2, low], b.g2, z2).wait_recv()


def tail_copy(r, i, y2, slot):
    return rcopy(
        r.xs.at[i, pl.ds(r.T - HALO, HALO)],
        r.xt.at[slot],
        r.sems[b.tail_s].at[i],
        r.sems[b.tail_r].at[slot],
        y2 * 2 + r.k + 1,
        r.c,
    )


def project(r):
    for i in range(1, r.nY + 1):
        y2 = lax.rem(r.y + i, r.nY)
        total = None
        for j in range(r.nX):
            term = dot(r.hg[j, y2], r.wp[j])
            total = term if total is None else total + term
        r.xs[i - 1] = total.astype(BF16)
        if i < r.nY:
            start(r, line_copy(r, i, r.xs.at[i - 1], r.xr.at[r.y], b.xr, r.y))
        start(r, tail_copy(r, i - 1, y2, r.y), y2 * 2 + r.k + 1 < r.nS)
    own = total

    @pl.when(r.s == 0)
    def _():
        r.xpad[pl.ds(0, HALO), :] = jnp.zeros((HALO, r.C), F32)

    @pl.when(r.s > 0)
    def _():
        tail = None
        for y2 in range(r.nY):
            tail_copy(r, 0, r.y, y2).wait_recv()
            term = r.xt[y2].astype(F32)
            tail = term if tail is None else tail + term
        r.xpad[pl.ds(0, HALO), :] = tail.astype(BF16).astype(F32)

    for i in range(1, r.nY):
        y2 = lax.rem(r.y + i, r.nY)
        line_copy(r, i, r.xs.at[i - 1], r.xr.at[y2], b.xr, y2).wait_recv()
        own = own + r.xr[y2].astype(F32)
    r.xpad[pl.ds(HALO, r.T), :] = own.astype(BF16).astype(F32)
    conv = jnp.zeros((r.T, r.C), F32) + r.conv_b[...]
    for k in range(r.KC):
        conv = conv + r.conv_w[k : k + 1, :] * r.xpad[pl.ds(HALO - r.KC + 1 + k, r.T), :]
    sig = jax.nn.sigmoid(conv)
    u = (conv * sig).astype(BF16)
    r.u[...] = u
    r.part[:, :, pl.ds(0, r.R)] = contract_last(u, r.w_delta_in[...]).reshape(r.nC, r.RP, r.R)
    r.part[:, :, pl.ds(r.R, 2 * r.N)] = contract_last(u, r.w_bc[...]).reshape(r.nC, r.RP, 2 * r.N)
    scatter_start(r, b.chan, r.part, r.part_r, b.p1)
    r.slope[...] = sig * (1.0 + conv * (1.0 - sig))
    r.part_a[r.c] = scatter_sum(r, b.chan, r.part, r.part_r, b.p1)
    gather_start(r, b.chan, r.part_a, b.p2)
    recv_wait(r, b.chan, r.part_a, b.p2)
    full = r.part_a[...].reshape(r.T, r.R + LANES)
    r.low[...] = full[:, : r.R].astype(BF16)
    r.bcw[...] = full[:, r.R :]


def wide(r, b):
    return jnp.concatenate([b] * (r.C // LANES), axis=1) if r.C > LANES else b


def block_mask(r, rows):
    row = lax.broadcasted_iota(jnp.int32, (rows, CH * r.N), 0)
    col = lax.broadcasted_iota(jnp.int32, (rows, CH * r.N), 1)
    return jnp.where(lax.rem(row, CH) == lax.div(col, r.N), 1.0, 0.0).astype(F32)


def pick(r):
    row = lax.broadcasted_iota(jnp.int32, (r.N, CH * r.N), 0)
    col = lax.broadcasted_iota(jnp.int32, (r.N, CH * r.N), 1)
    return jnp.where(lax.rem(col, r.N) == row, 1.0, 0.0).astype(F32)


def prepare(r):
    pre = dot(r.low[...], r.w_dt[...]) + r.dt_bias[...]
    r.pre[...] = pre
    delta = softplus(pre)
    r.delta[...] = delta
    r.sd[...] = jnp.sum(delta, 0, keepdims=True)
    for i, j, dev in peers(r, b.seq):
        start(r, rcopy(r.sd, r.sd_r.at[r.s], r.sems[b.sd_s].at[i], r.sems[b.sd_r].at[r.s], *dev))
    u = r.u[...].astype(F32)
    r.du[...] = delta * u
    turned = r.bcw[...].T
    for t in range(r.T):
        r.bx[t] = jnp.broadcast_to(turned[0 : r.N, t : t + 1], (r.N, LANES))
        r.cx[t] = jnp.broadcast_to(turned[r.N : 2 * r.N, t : t + 1], (r.N, LANES))


def forward(r, init, full):
    a_mat = r.am[...]
    if full:
        mask = block_mask(r, CH)
        r.hh[pl.ds(0, r.N), :] = init

    def chunk(j, h):
        base = pl.multiple_of(j * CH, CH)
        d = r.delta[pl.ds(base, CH), :]
        du = r.du[pl.ds(base, CH), :]
        kept = []
        for t in range(CH):
            at = pl.multiple_of((base + t) * r.N, r.N)
            if full:
                a = r.aa[pl.ds(at, r.N), :]
            else:
                a = jnp.exp(d[t : t + 1, :] * a_mat)
                r.aa[pl.ds(at, r.N), :] = a
            h = a * h + du[t : t + 1, :] * wide(r, r.bx[base + t])
            if full:
                r.hh[pl.ds(at + r.N, r.N), :] = h
                kept.append(h.astype(BF16))
        if full:
            rows = jnp.concatenate(kept, 0)
            r.y_scan[pl.ds(base, CH), :] = dot(r.cd[pl.ds(base, CH), :], rows)
            r.cm[pl.ds(base, CH), :] = mask * contract_last(r.g[pl.ds(base, CH), :].astype(BF16), rows)
        return h

    return lax.fori_loop(0, r.T // CH, chunk, init)


def backward(r, init, full):
    a_mat = r.am[...]
    mask = block_mask(r, CH)
    chunks = r.T // CH

    def chunk(i, carry):
        base = pl.multiple_of((chunks - 1 - i) * CH, CH)
        kap, acc = carry
        d = r.delta[pl.ds(base, CH), :]
        g = r.g[pl.ds(base, CH), :]
        lams, qas = [None] * CH, [None] * CH
        for t in reversed(range(CH)):
            at = pl.multiple_of((base + t) * r.N, r.N)
            lam = kap + wide(r, r.cx[base + t]) * g[t : t + 1, :]
            kap = r.aa[pl.ds(at, r.N), :] * lam
            if full:
                q = kap * r.hh[pl.ds(at, r.N), :]
                acc = acc + q * d[t : t + 1, :]
                qas[t] = (q * a_mat).astype(BF16)
                lams[t] = lam.astype(BF16)
        if full:
            lam_rows = jnp.concatenate(lams, 0)
            du = r.du[pl.ds(base, CH), :]
            r.s1[pl.ds(base, CH), :] = dot(r.bd[pl.ds(base, CH), :], lam_rows)
            r.s2[pl.ds(base, CH), :] = dot(mask.astype(BF16), jnp.concatenate(qas, 0))
            r.bm[pl.ds(base, CH), :] = mask * contract_last(du.astype(BF16), lam_rows)
        return kap, acc

    return lax.fori_loop(0, chunks, chunk, (init, jnp.zeros_like(init)))


def state_copy(r, which, j, slot):
    return rcopy(r.ef.at[which], r.st_r.at[slot], r.sems[b.st_s].at[j], r.sems[b.st_r].at[slot], j, r.c)


def scan(r):
    zero = jnp.zeros((r.N, r.C), F32)
    r.ef[0] = forward(r, zero, False).astype(BF16)
    for j in range(1, r.nS):
        start(r, state_copy(r, 0, j, r.s), j > r.s)
    r.ef[1] = backward(r, zero, False)[0].astype(BF16)
    for j in range(r.nS - 1):
        start(r, state_copy(r, 1, j, r.s), j < r.s)
    picked = pick(r)
    tall = block_mask(r, r.T)
    r.bd[...] = (tall * dot(r.bcw[:, pl.ds(0, r.N)], picked)).astype(BF16)
    r.cd[...] = (tall * dot(r.bcw[:, pl.ds(r.N, r.N)], picked)).astype(BF16)

    def enter(j, into):
        rcopy(r.sd, r.sd_r.at[j], r.sems[b.sd_s].at[0], r.sems[b.sd_r].at[j], j, r.c).wait_recv()
        state_copy(r, 0, j, j).wait_recv()
        into[...] = jnp.exp(r.am[...] * r.sd_r[j]) * into[...] + r.st_r[j].astype(F32)

    r.h_in[...] = zero
    for j in range(r.nS - 1):
        pl.when(j < r.s)(functools.partial(enter, j, r.h_in))
    forward(r, r.h_in[...], True)
    r.l_in[...] = zero
    for j in range(r.nS - 1, 0, -1):
        pl.when(j > r.s)(functools.partial(enter, j, r.l_in))
    a_adj = backward(r, r.l_in[...], True)[1]
    s1 = r.s1[...]
    u = r.u[...].astype(F32)
    pre_adj = ((u * s1 + r.s2[...]) * jax.nn.sigmoid(r.pre[...])).astype(BF16)
    exact = lax.Precision.HIGHEST
    nt = (((1,), (1,)), ((), ()))
    b_adj = lax.dot_general(r.bm[...], picked, nt, precision=exact, preferred_element_type=F32)
    c_adj = lax.dot_general(r.cm[...], picked, nt, precision=exact, preferred_element_type=F32)
    r.part2[:, :, pl.ds(0, r.R)] = contract_last(pre_adj, r.w_dt[...]).reshape(r.nC, r.RP, r.R)
    r.part2[:, :, pl.ds(r.R, r.N)] = b_adj.reshape(r.nC, r.RP, r.N)
    r.part2[:, :, pl.ds(r.R + r.N, r.N)] = c_adj.reshape(r.nC, r.RP, r.N)
    scatter_start(r, b.chan, r.part2, r.part2_r, b.p3)
    r.dt_p[...] = contract_first(r.low[...], pre_adj).astype(BF16).reshape(2, r.nY, r.R // r.nS, r.C)
    start(r, pair_copy(r, r.dt_p.at[1 - r.k], r.dt_b, b.d1))
    alog = (a_adj * r.am[...]).astype(BF16)
    wide_half = r.C // 2
    for j in range(2):
        r.mi_p[j, pl.ds(2 * r.N, r.N), :] = alog[:, j * wide_half : (j + 1) * wide_half]
    skip = r.skip_d[...]
    r.uu[...] = r.delta[...] * s1 + skip * r.g[...]
    r.gate_out[...] = (r.gs[...] * (r.y_scan[...] + skip * u)).astype(BF16)


def grad_copy(r, i, j):
    y2, x2 = lax.rem(r.y + i, r.nY), lax.rem(r.x + j, r.nX)
    n = i * r.nX + j
    return rcopy(
        r.hs.at[n], r.hr.at[r.c], r.sems[b.hg_s].at[n], r.sems[b.hg_r].at[r.c], y2 * 2 + r.k, r.y * r.nX + x2
    )


def weight_pair(r, part, got, summed, key):
    pair_copy(r, part.at[1 - r.k], got, key[0]).wait_recv()
    summed[...] = (part[r.k].astype(F32) + got[...].astype(F32)).astype(BF16)


def weight_line(r, summed, got, whole, keys):
    total = summed[r.y].astype(F32)
    for i in range(1, r.nY):
        y2 = lax.rem(r.y + i, r.nY)
        line_copy(r, i, summed.at[y2], got.at[y2], keys[0], y2).wait_recv()
        total = total + got[y2].astype(F32)
    whole[r.k, r.y] = total.astype(BF16)
    for i in range(1, r.nY):
        start(r, line_copy(r, i, whole.at[r.k, r.y], whole.at[r.k, r.y], keys[1], r.y))


def weight_back(r, whole, line_key, pair_key):
    for i in range(1, r.nY):
        y2 = lax.rem(r.y + i, r.nY)
        line_copy(r, i, whole.at[r.k, y2], whole.at[r.k, y2], line_key, y2).wait_recv()
    start(r, pair_copy(r, whole.at[r.k], whole.at[r.k], pair_key))


def weight_end(r, whole, pair_key):
    pair_copy(r, whole.at[r.k], whole.at[1 - r.k], pair_key).wait_recv()


def spread(r, summed, got, key):
    for i in range(1, r.nY):
        start(r, line_copy(r, i, summed.at[lax.rem(r.y + i, r.nY)], got.at[r.y], key, r.y))


def gradients(r):
    half = r.nX // 2
    wide_half = r.C // 2
    flush(r)
    r.part2_a[r.c] = scatter_sum(r, b.chan, r.part2, r.part2_r, b.p3)
    gather_start(r, b.chan, r.part2_a, b.p4)
    weight_pair(r, r.dt_p, r.dt_b, r.dt_c, (b.d1,))
    spread(r, r.dt_c, r.dt_d, b.d2)
    recv_wait(r, b.chan, r.part2_a, b.p4)
    full = r.part2_a[...].reshape(r.T, r.R + LANES)
    low_adj = full[:, : r.R].astype(BF16)
    bc_adj = full[:, r.R : r.R + 2 * r.N].astype(BF16)
    u_adj = r.uu[...] + dot(low_adj, r.w_delta_in[...]) + dot(bc_adj, r.w_bc[...])
    conv_adj = u_adj * r.slope[...]
    r.cpad[pl.ds(0, r.T), :] = conv_adj

    def head_copy(to):
        return rcopy(
            r.cpad.at[pl.ds(0, HEAD)],
            r.cpad.at[pl.ds(r.T, HEAD)],
            r.sems[b.head_s].at[0],
            r.sems[b.head_r].at[0],
            to,
            r.c,
        )

    start(r, head_copy(r.s - 1), r.s > 0)

    @pl.when(r.s == r.nS - 1)
    def _():
        r.cpad[pl.ds(r.T, HEAD), :] = jnp.zeros((HEAD, r.C), F32)

    def x_adj(first, count):
        rows = pl.ds(first, count)
        total = jnp.zeros((count, r.C), F32)
        for k in range(r.KC):
            total = total + r.conv_w[k : k + 1, :] * r.cpad[pl.ds(first + r.KC - 1 - k, count), :]
        r.xg[r.y, rows] = total.astype(BF16)

    def x_copy(i, slot, part):
        rows = pl.ds(0, r.T - HALO) if part == 0 else pl.ds(r.T - HALO, HALO)
        return line_copy(r, i, r.xg.at[slot, rows], r.xg.at[slot, rows], b.xg, slot, part)

    x_adj(0, r.T - HALO)
    for i in range(1, r.nY):
        start(r, x_copy(i, r.y, 0))
    u = r.u[...]
    r.di_p[...] = contract_first(low_adj, u).astype(BF16).reshape(2, r.nY, r.R // r.nS, r.C)
    start(r, pair_copy(r, r.di_p.at[1 - r.k], r.di_b, b.d5))
    bc_term = contract_first(bc_adj, u).astype(BF16)
    for j in range(2):
        r.mi_p[j, pl.ds(0, 2 * r.N), :] = bc_term[:, j * wide_half : (j + 1) * wide_half]
    start(r, pair_copy(r, r.mi_p.at[1 - r.k], r.mi_b, b.m1))
    weight_line(r, r.dt_c, r.dt_d, r.dt_e, (b.d2, b.d3))

    pl.when(r.s < r.nS - 1)(lambda: head_copy(r.s + 1).wait_recv())
    x_adj(r.T - HALO, HALO)
    for i in range(1, r.nY):
        start(r, x_copy(i, r.y, 1))

    for i in range(r.nY):
        y2 = lax.rem(r.y + i, r.nY)
        if i:
            x_copy(i, y2, 0).wait_recv()
            x_copy(i, y2, 1).wait_recv()
        for j in range(r.nX):
            x2 = lax.rem(r.x + j, r.nX)
            n = i * r.nX + j
            r.hs[n] = contract_last(r.xg[y2], r.wp[x2]).astype(BF16)
            if n == 0:

                @pl.when(r.y == r.z)
                def _():
                    r.hr[r.c] = r.hs[0]

                start(r, grad_copy(r, 0, 0), r.y != r.z)
            else:
                start(r, grad_copy(r, i, j))
        if i == 0:
            weight_pair(r, r.di_p, r.di_b, r.di_c, (b.d5,))
            spread(r, r.di_c, r.di_d, b.d6)
            pair_copy(r, r.mi_p.at[1 - r.k], r.mi_b, b.m1).wait_recv()
            r.mi_c[r.y] = (r.mi_p[r.k].astype(F32) + r.mi_b[...].astype(F32)).astype(BF16)
            for i2 in range(1, r.nY):
                start(r, line_copy(r, i2, r.mi_c.at[r.y], r.mi_c.at[r.y], b.m2, r.y))
        if i == 1:
            weight_back(r, r.dt_e, b.d3, b.d4)

    x_all = r.xg[...].reshape(r.nY * r.T, r.C)

    def weight(x2):
        return contract_first(r.hg[x2].reshape(r.nY * r.T, r.DH), x_all)

    for j in range(half):
        r.ws[j] = weight((1 - r.k) * half + j).astype(BF16)
    start(r, pair_copy(r, r.ws, r.wr, b.wg))
    weight_line(r, r.di_c, r.di_d, r.di_e, (b.d6, b.d7))
    total = r.mi_c[r.y].astype(F32)
    for i in range(1, r.nY):
        y2 = lax.rem(r.y + i, r.nY)
        line_copy(r, i, r.mi_c.at[y2], r.mi_c.at[y2], b.m2, y2).wait_recv()
        total = total + r.mi_c[y2].astype(F32)
    r.mi_e[r.k] = total
    start(r, pair_copy(r, r.mi_e.at[r.k], r.mi_e.at[r.k], b.m3))
    for j in range(half):
        r.wo[j] = weight(r.k * half + j)
    pair_copy(r, r.ws, r.wr, b.wg).wait_recv()
    r.w_out[...] = (r.wo[...] + r.wr[...].astype(F32)).astype(BF16)
    weight_back(r, r.di_e, b.d7, b.d8)
    weight_end(r, r.dt_e, b.d4)
    pair_copy(r, r.mi_e.at[r.k], r.mi_e.at[1 - r.k], b.m3).wait_recv()
    total = None
    for j in range(r.nC):
        c2 = lax.rem(r.c + j, r.nC)
        wait = rcopy(
            r.hs.at[0], r.hr.at[c2], r.sems[b.hg_s].at[0], r.sems[b.hg_r].at[c2], r.z * 2 + r.k, c2
        )
        if j == 0:
            pl.when(r.y != r.z)(lambda wait=wait: wait.wait_recv())
        else:
            wait.wait_recv()
        term = r.hr[c2].astype(F32)
        total = term if total is None else total + term
    r.hidden_out[...] = total.astype(BF16)
    weight_end(r, r.di_e, b.d8)
    flush(r)


def finish(r):
    scale = 1.0 / math.sqrt(r.T * r.nS)
    wide_half = r.C // 2
    r.hidden_grad[...] = r.hidden_out[...]
    r.gate_grad[...] = r.gate_out[...]
    r.w_in_grad[...] = r.w_out[...].astype(F32) * scale
    r.w_dt_grad[...] = r.dt_e[...].astype(F32).reshape(r.R, r.C) * scale
    r.w_delta_in_grad[...] = r.di_e[...].astype(F32).reshape(r.R, r.C) * scale
    for j in range(2):
        cols = pl.ds(j * wide_half, wide_half)
        r.w_bc_grad[:, cols] = r.mi_e[j, pl.ds(0, 2 * r.N), :] * scale
        r.a_log_grad[:, cols] = r.mi_e[j, pl.ds(2 * r.N, r.N), :] * scale


def tables(dim):
    d = types.SimpleNamespace(**dim)
    t, c, n, rows, q = d.T, d.C, d.N, d.R, d.R // d.nS
    wide_row = rows + LANES
    buffers = dict(
        hg=((d.nX, d.nY, t, d.DH), BF16),
        wp=((d.nX, d.DH, c), BF16),
        xs=((d.nY, t, c), BF16),
        xr=((d.nY, t, c), BF16),
        xt=((d.nY, HALO, c), BF16),
        xpad=((HALO + t, c), F32),
        slope=((t, c), F32),
        gs=((t, c), F32),
        u=((t, c), BF16),
        part=((d.nC, d.RP, wide_row), F32),
        part_r=((d.nC, d.RP, wide_row), F32),
        part_a=((d.nC, d.RP, wide_row), F32),
        low=((t, rows), BF16),
        bcw=((t, LANES), F32),
        pre=((t, c), F32),
        delta=((t, c), F32),
        du=((t, c), F32),
        g=((t, c), F32),
        am=((n, c), F32),
        bx=((t, n, LANES), F32),
        cx=((t, n, LANES), F32),
        sd=((1, c), F32),
        aa=((t * n, c), F32),
        hh=(((t + 1) * n, c), F32),
        ef=((2, n, c), BF16),
        st_r=((d.nS, n, c), BF16),
        sd_r=((d.nS, 1, c), F32),
        h_in=((n, c), F32),
        l_in=((n, c), F32),
        bd=((t, CH * n), BF16),
        cd=((t, CH * n), BF16),
        bm=((t, CH * n), F32),
        cm=((t, CH * n), F32),
        y_scan=((t, c), F32),
        s1=((t, c), F32),
        s2=((t, c), F32),
        uu=((t, c), F32),
        part2=((d.nC, d.RP, wide_row), F32),
        part2_r=((d.nC, d.RP, wide_row), F32),
        part2_a=((d.nC, d.RP, wide_row), F32),
        dt_p=((2, d.nY, q, c), BF16),
        dt_b=((d.nY, q, c), BF16),
        dt_c=((d.nY, q, c), BF16),
        dt_d=((d.nY, q, c), BF16),
        dt_e=((2, d.nY, q, c), BF16),
        di_p=((2, d.nY, q, c), BF16),
        di_b=((d.nY, q, c), BF16),
        di_c=((d.nY, q, c), BF16),
        di_d=((d.nY, q, c), BF16),
        di_e=((2, d.nY, q, c), BF16),
        mi_p=((2, 3 * n, c // 2), BF16),
        mi_b=((3 * n, c // 2), BF16),
        mi_c=((d.nY, 3 * n, c // 2), BF16),
        mi_e=((2, 3 * n, c // 2), F32),
        cpad=((t + HEAD, c), F32),
        xg=((d.nY, t, c), BF16),
        hs=((d.nC, t, d.DH), BF16),
        hr=((d.nC, t, d.DH), BF16),
        ws=((d.nX // 2, d.DH, c), BF16),
        wr=((d.nX // 2, d.DH, c), BF16),
        wo=((d.nX // 2, d.DH, c), F32),
        w_out=((d.nX // 2, d.DH, c), BF16),
        hidden_out=((t, d.DH), BF16),
        gate_out=((t, c), BF16),
        hidden_grad=((t, d.DH), BF16),
        gate_grad=((t, c), BF16),
        w_in_grad=((d.nX // 2, d.DH, c), F32),
        w_delta_in_grad=((rows, c), F32),
        w_bc_grad=((2 * n, c), F32),
        w_dt_grad=((rows, c), F32),
        a_log_grad=((n, c), F32),
    )
    sems = dict(loc=1)
    pairs = (b.tu, b.wp, b.head, b.wg, b.d1, b.d4, b.d5, b.d8, b.m1, b.m3)
    lines = (b.xr, b.tail, b.d2, b.d3, b.d6, b.d7, b.m2)
    for key in pairs:
        sems[key + "_s"] = sems[key + "_r"] = 1
    for key in lines:
        sems[key + "_s"] = sems[key + "_r"] = d.nY
    sems[b.xg_s] = sems[b.xg_r] = 2 * d.nY
    for key in (b.g1, b.g2):
        sems[key + "_s"] = sems[key + "_r"] = d.nX + d.nY
    for key in (b.hg, b.p1, b.p2, b.p3, b.p4):
        sems[key + "_s"] = sems[key + "_r"] = d.nC
    for key in (b.st, b.sd):
        sems[key + "_s"] = sems[key + "_r"] = d.nS
    return buffers, sems


def run(dim, phases, groups, values, ins, outs, scratch, sem_names, number, cost):
    buffers, sem_sizes = tables(dim)

    def body(*refs):
        r = types.SimpleNamespace(**dim)
        for name, ref in zip(ins + outs + scratch, refs):
            setattr(r, name, ref)
        r.sems = dict(zip(sem_names, refs[len(ins) + len(outs) + len(scratch) :]))
        r.sent = []
        if groups:
            r.s, r.c = lax.axis_index(b.seq), lax.axis_index(b.chan)
            r.y, r.k = lax.div(r.s, 2), lax.rem(r.s, 2)
            r.z, r.x = lax.div(r.c, r.nX), lax.rem(r.c, r.nX)
            greet(r, groups)
        for phase in phases:
            phase(r)

    space = pl.BlockSpec(memory_space=pltpu.VMEM)
    extra = dict(collective_id=number, has_side_effects=True) if groups else {}
    results = pl.pallas_call(
        body,
        out_shape=[jax.ShapeDtypeStruct(*buffers[name]) for name in outs],
        in_specs=[space] * len(ins),
        out_specs=[space] * len(outs),
        scratch_shapes=[pltpu.VMEM(*buffers[name]) for name in scratch]
        + [pltpu.SemaphoreType.DMA((sem_sizes[name],)) for name in sem_names],
        compiler_params=pltpu.CompilerParams(vmem_limit_bytes=56 << 20, **extra),
        cost_estimate=pl.CostEstimate(flops=cost, bytes_accessed=4 << 20, transcendentals=0),
        name=phases[0].__name__,
    )(*[values[name] for name in ins])
    values.update(zip(outs, results))


ORDER = [b.hidden_grad, b.gate_grad, b.w_in_grad, b.w_delta_in_grad, b.w_bc_grad, b.w_dt_grad, b.a_log_grad]


def per_device(
    seq, chan, hidden, gate_in, out_grad, w_in, conv_w, conv_b, w_delta_in, w_bc, w_dt, dt_bias, a_log, skip_d
):
    lines = seq // 2
    dim = dict(
        nS=seq,
        nC=chan,
        nY=lines,
        nX=chan // lines,
        T=hidden.shape[0],
        DH=hidden.shape[1],
        C=w_in.shape[1],
        R=w_delta_in.shape[0],
        N=a_log.shape[0],
        KC=conv_w.shape[0],
        RP=hidden.shape[0] // chan,
    )
    v = dict(
        hidden=hidden,
        gate_in=gate_in,
        out_grad=out_grad,
        w_in=w_in.reshape(dim[b.nX] // 2, dim[b.DH], dim[b.C]),
        conv_w=conv_w,
        conv_b=conv_b[None],
        w_delta_in=w_delta_in,
        w_bc=w_bc,
        w_dt=w_dt,
        dt_bias=dt_bias[None],
        a_log=a_log,
        skip_d=skip_d[None],
    )
    raw = [b.hidden_out, b.gate_out, b.w_out, b.dt_e, b.di_e, b.mi_e]
    given = list(v)
    buffers, sems = tables(dim)
    scratch = [name for name in buffers if name not in given + raw + ORDER]
    run(dim, [take_hidden, project, prepare, scan, gradients], [b.cross, b.chan, b.seq], v, given, raw, scratch, list(sems), 0, 2_000_000_000)
    run(dim, [finish], [], v, raw, ORDER, [], [], 0, 1_000_000)
    v[b.w_in_grad] = v[b.w_in_grad].reshape(w_in.shape)
    return tuple(v[name] for name in ORDER)


def solution(mesh):
    placed = (
        P(b.seq, b.chan),
        P(b.seq, b.chan),
        P(b.seq, b.chan),
        P(b.seq, b.chan),
        P(None, b.chan),
        P(b.chan),
        P(None, b.chan),
        P(None, b.chan),
        P(None, b.chan),
        P(b.chan),
        P(None, b.chan),
        P(b.chan),
    )
    return jax.shard_map(
        functools.partial(per_device, mesh.shape[b.seq], mesh.shape[b.chan]),
        mesh=mesh,
        in_specs=placed,
        out_specs=(
            P(b.seq, b.chan),
            P(b.seq, b.chan),
            P(b.seq, b.chan),
            P(None, b.chan),
            P(None, b.chan),
            P(None, b.chan),
            P(None, b.chan),
        ),
        check_vma=False,
    )
```

time: 174 us -> 103 us (0.59)
  Pallas kernels: 166 us -> 102 us
  local copies, waits for them, and re-layouts: 6.7 us -> 0 us
    pallas_call x5 -> x2, Pallas kernels: 166 us -> 102 us  [run(): pl.pallas_call(body, out_shape=[jax.ShapeDtypeStruct(*buffers[name]) for...]
    unnamed x14 -> x0, local copies, waits for them, and re-layouts: 6.7 us -> none
where the time goes in v2:
time: 103 us
  Pallas kernels  102 us (99%)
    pallas_call x2, Pallas kernels, run(): pl.pallas_call(body, out_shape=[jax.ShapeDtypeStruct(*buffers[name]) for...  102 us

profile of v2, /device:TPU:1, one launch (start us, length us, event | category | flops | bytes accessed | tf_op | source)
XLA Modules:
  0.0 102.6 jit_solution(5181633504032332021)
XLA Ops:
  0.6 99.3 %take_hidden.1 = (bf16[128,256]{1,0:T(8,128)(2,1)}, bf16[128,512]{1,0:T(8,128)(2,1)}, bf16[2,256,512]{2,1,0:T(8,128)(2,1)}, bf16[2,4,32,512]{3,2,1,0:T(8,128)(2,...) custom-call(bf16[128,256]{1,0:T(8,128)(2,1)} %refs_0_.1, bf16[128,512]{1,0:T(8,128)(2,1)} %refs_1_.1, ...), custom_call_target="tpu_custom_call" | custom-call | flops 2000000000 | bytes 4194304 | tf_op jit(solution)/shard_map/take_hidden/pallas_call | solution.py:720
  99.9 2.7 %finish.1 = (bf16[128,256]{1,0:T(8,128)(2,1)}, bf16[128,512]{1,0:T(8,128)(2,1)}, f32[2,256,512]{2,1,0:T(8,128)}, f32[256,512]{1,0:T(8,128)}, f32[32,512]{1,0:T(8...) custom-call(bf16[128,256]{1,0:T(8,128)(2,1)} %get-tuple-element.20.refs_0_, bf16[128,512]{1,0:T(8,128)(2,1)} %get-tuple-element.21.refs_1_, ...), custom_call_target="tpu_custom_call" | custom-call | flops 1000000 | bytes 4194304 | tf_op jit(solution)/shard_map/finish/pallas_call | solution.py:720

commit v3 on v2

--- a/solution.py
+++ b/solution.py
@@ -135,52 +135,77 @@
     return rcopy(src, dst, r.sems[key + "_s"].at[at + i], r.sems[key + "_r"].at[at + slot], seq, chan)
 
 
-def greet(r, groups):
+def greet(r, during):
     barrier = pltpu.get_barrier_semaphore()
-    count = 0
 
     def tell(seq, chan):
         pl.semaphore_signal(barrier, inc=1, device_id=dict(seq=seq, chan=chan), device_id_type=MESH)
 
-    for group in groups:
-        if group in (b.seq, b.chan):
-            for i, j, dev in peers(r, group):
-                tell(*dev)
-                count += 1
-        elif group == b.cross:
-            for i in range(r.nC):
-                c2 = lax.rem(r.c + i, r.nC)
-                if i == 0:
-                    pl.when(r.y != r.z)(lambda c2=c2: tell(r.z * 2 + r.k, c2))
-                else:
-                    tell(r.z * 2 + r.k, c2)
-            for i in range(r.nY):
-                for j in range(r.nX):
-                    y2, x2 = lax.rem(r.y + i, r.nY), lax.rem(r.x + j, r.nX)
-                    if i == 0 and j == 0:
-                        pl.when(r.y != r.z)(lambda y2=y2, x2=x2: tell(y2 * 2 + r.k, r.y * r.nX + x2))
-                    else:
-                        tell(y2 * 2 + r.k, r.y * r.nX + x2)
-            count += 2 * (r.nC - 1)
-    if b.cross in groups:
-        apart = (r.y - r.z) * (r.y - r.z)
-        count = count + 2 * lax.div(apart + r.nY * r.nY - 1, r.nY * r.nY)
-    pl.semaphore_wait(barrier, count)
+    pl.when(r.y != r.z)(lambda: tell(r.z * 2 + r.k, r.y * r.nX + r.x))
+    for i in range(1, r.nX):
+        tell(r.s, r.z * r.nX + lax.rem(r.x + i, r.nX))
+        tell(r.s, lax.rem(r.z + i, r.nY) * r.nX + r.x)
+    for i, j, dev in peers(r, b.seq):
+        tell(*dev)
+    during()
+    apart = (r.y - r.z) * (r.y - r.z)
+    apart = lax.div(apart + r.nY * r.nY - 1, r.nY * r.nY)
+    pl.semaphore_wait(barrier, 2 * (r.nX - 1) + r.nS - 1 + apart)
+
+
+def load(r):
+    for at, (name, ref) in enumerate(r.given.items()):
+        if name in (b.w_in, b.hidden):
+            continue
+        pltpu.make_async_copy(ref, getattr(r, name), r.sems[b.inp].at[at]).start()
+
+
+def need(r, *names):
+    for name in names:
+        at = list(r.given).index(name)
+        pltpu.make_async_copy(r.given[name], getattr(r, name), r.sems[b.inp].at[at]).wait()
+
+
+def weight_rows(r, y2, core, part):
+    half, cut = r.nX // 2, r.DH // 2
+    return r.wf.at[y2, pl.ds(core * half, half), pl.ds(part * cut, cut)]
+
+
+def weight_copy(r, i, y2, part):
+    rows = weight_rows(r, y2, r.k, part)
+    return line_copy(r, i, rows, rows, b.wy, y2, part)
+
+
+def relay_copy(r, i, y2, core, part):
+    rows, at = weight_rows(r, y2, core, part), part * r.nY + i
+    return rcopy(rows, rows, r.sems[b.wz_s].at[at], r.sems[b.wz_r].at[at], r.y * 2 + 1 - r.k, r.c)
+
+
+def weight_send(r, part):
+    for i in range(1, r.nY):
+        start(r, weight_copy(r, i, r.y, part))
+
+
+def weight_relay(r, part):
+    for i in range(1, r.nY):
+        y2 = lax.rem(r.y + i, r.nY)
+        weight_copy(r, i, y2, part).wait_recv()
+        start(r, relay_copy(r, i, y2, r.k, part))
 
 
 def take_hidden(r):
     half, cut = r.nX // 2, r.T // 2
-    own_w = pltpu.make_async_copy(r.w_in, r.wp.at[pl.ds(r.k * half, half)], r.sems[b.loc].at[0])
-    own_w.start()
+    mine = r.wf.at[r.y, pl.ds(r.k * half, half)]
+    own_w = pltpu.make_async_copy(r.w_in, mine, r.sems[b.loc].at[0])
+    own_h = pltpu.make_async_copy(r.hidden, r.hg.at[r.x, r.y], r.sems[b.loc].at[1])
     turn = rcopy(
         r.hidden, r.hg.at[r.x, r.y], r.sems[b.tu_s].at[0], r.sems[b.tu_r].at[0], r.z * 2 + r.k, r.y * r.nX + r.x
     )
     start(r, turn, r.y != r.z)
-    start(r, pair_copy(r, r.w_in, r.wp.at[pl.ds(r.k * half, half)], b.wp))
-
-    @pl.when(r.y == r.z)
-    def _():
-        r.hg[r.x, r.y] = r.hidden[...]
+    start(r, pair_copy(r, r.w_in, mine, b.wp))
+    own_w.start()
+    pl.when(r.y == r.z)(own_h.start)
+    need(r, b.gate_in, b.out_grad, b.a_log)
 
     gate = r.gate_in[...].astype(F32)
     sig = jax.nn.sigmoid(gate)
@@ -191,6 +216,7 @@
     r.part[:, :, pl.ds(r.R, LANES)] = jnp.zeros((r.nC, r.RP, LANES), F32)
     r.part2[:, :, pl.ds(r.R, LANES)] = jnp.zeros((r.nC, r.RP, LANES), F32)
     own_w.wait()
+    pl.when(r.y == r.z)(own_h.wait)
 
     @pl.when(r.y != r.z)
     def _():
@@ -202,6 +228,7 @@
     for i in range(1, r.nX):
         start(r, plane_copy(r, i, True, r.hg.at[r.x, r.z, low], r.hg.at[r.x, r.z, low], b.g1, r.x))
         start(r, plane_copy(r, i, False, r.hg.at[r.x, r.z, high], r.hg.at[r.x, r.z, high], b.g1, r.z))
+    weight_send(r, 0)
     for i in range(1, r.nX):
         x2, z2 = lax.rem(r.x + i, r.nX), lax.rem(r.z + i, r.nY)
         plane_copy(r, i, True, r.hg.at[x2, r.z, low], r.hg.at[x2, r.z, low], b.g1, x2).wait_recv()
@@ -209,7 +236,7 @@
     for i in range(1, r.nX):
         start(r, plane_copy(r, i, False, r.hg.at[:, r.z, low], r.hg.at[:, r.z, low], b.g2, r.z))
         start(r, plane_copy(r, i, True, r.hg.at[r.x, :, high], r.hg.at[r.x, :, high], b.g2, r.x))
-    pair_copy(r, r.w_in, r.wp.at[pl.ds((1 - r.k) * half, half)], b.wp).wait_recv()
+    pair_copy(r, r.w_in, r.wf.at[r.y, pl.ds((1 - r.k) * half, half)], b.wp).wait_recv()
     for i in range(1, r.nX):
         x2, z2 = lax.rem(r.x + i, r.nX), lax.rem(r.z + i, r.nY)
         plane_copy(r, i, True, r.hg.at[x2, :, high], r.hg.at[x2, :, high], b.g2, x2).wait_recv()
@@ -232,7 +259,7 @@
         y2 = lax.rem(r.y + i, r.nY)
         total = None
         for j in range(r.nX):
-            term = dot(r.hg[j, y2], r.wp[j])
+            term = dot(r.hg[j, y2], r.wf[r.y, j])
             total = term if total is None else total + term
         r.xs[i - 1] = total.astype(BF16)
         if i < r.nY:
@@ -258,6 +285,7 @@
         line_copy(r, i, r.xs.at[i - 1], r.xr.at[y2], b.xr, y2).wait_recv()
         own = own + r.xr[y2].astype(F32)
     r.xpad[pl.ds(HALO, r.T), :] = own.astype(BF16).astype(F32)
+    need(r, b.conv_w, b.conv_b, b.w_delta_in, b.w_bc)
     conv = jnp.zeros((r.T, r.C), F32) + r.conv_b[...]
     for k in range(r.KC):
         conv = conv + r.conv_w[k : k + 1, :] * r.xpad[pl.ds(HALO - r.KC + 1 + k, r.T), :]
@@ -267,6 +295,8 @@
     r.part[:, :, pl.ds(0, r.R)] = contract_last(u, r.w_delta_in[...]).reshape(r.nC, r.RP, r.R)
     r.part[:, :, pl.ds(r.R, 2 * r.N)] = contract_last(u, r.w_bc[...]).reshape(r.nC, r.RP, 2 * r.N)
     scatter_start(r, b.chan, r.part, r.part_r, b.p1)
+    weight_send(r, 1)
+    weight_relay(r, 0)
     r.slope[...] = sig * (1.0 + conv * (1.0 - sig))
     r.part_a[r.c] = scatter_sum(r, b.chan, r.part, r.part_r, b.p1)
     gather_start(r, b.chan, r.part_a, b.p2)
@@ -293,6 +323,7 @@
 
 
 def prepare(r):
+    need(r, b.w_dt, b.dt_bias, b.skip_d)
     pre = dot(r.low[...], r.w_dt[...]) + r.dt_bias[...]
     r.pre[...] = pre
     delta = softplus(pre)
@@ -411,6 +442,7 @@
     r.part2[:, :, pl.ds(r.R, r.N)] = b_adj.reshape(r.nC, r.RP, r.N)
     r.part2[:, :, pl.ds(r.R + r.N, r.N)] = c_adj.reshape(r.nC, r.RP, r.N)
     scatter_start(r, b.chan, r.part2, r.part2_r, b.p3)
+    weight_relay(r, 1)
     r.dt_p[...] = contract_first(r.low[...], pre_adj).astype(BF16).reshape(2, r.nY, r.R // r.nS, r.C)
     start(r, pair_copy(r, r.dt_p.at[1 - r.k], r.dt_b, b.d1))
     alog = (a_adj * r.am[...]).astype(BF16)
@@ -422,12 +454,23 @@
     r.gate_out[...] = (r.gs[...] * (r.y_scan[...] + skip * u)).astype(BF16)
 
 
-def grad_copy(r, i, j):
-    y2, x2 = lax.rem(r.y + i, r.nY), lax.rem(r.x + j, r.nX)
-    n = i * r.nX + j
+def grad_copy(r, i, part):
+    rows = pl.ds(part * (r.T // 2), r.T // 2)
+    c2 = lax.rem(r.c + i, r.nC)
+    at = part * r.nC
     return rcopy(
-        r.hs.at[n], r.hr.at[r.c], r.sems[b.hg_s].at[n], r.sems[b.hg_r].at[r.c], y2 * 2 + r.k, r.y * r.nX + x2
-    )
+        r.hs.at[i, rows], r.hr.at[r.c, rows], r.sems[b.hg_s].at[at + i], r.sems[b.hg_r].at[at + r.c], r.s, c2
+    )
+
+
+def grad_part(r, part):
+    rows = pl.ds(part * (r.T // 2), r.T // 2)
+    for i in range(r.nC - 1, -1, -1):
+        c2 = lax.rem(r.c + i, r.nC)
+        term = contract_last(r.xg[r.y, rows], r.wf[lax.div(c2, r.nX), lax.rem(c2, r.nX)])
+        r.hs[i, rows] = term.astype(BF16)
+        if i:
+            start(r, grad_copy(r, i, part))
 
 
 def weight_pair(r, part, got, summed, key):
@@ -502,12 +545,16 @@
         r.xg[r.y, rows] = total.astype(BF16)
 
     def x_copy(i, slot, part):
-        rows = pl.ds(0, r.T - HALO) if part == 0 else pl.ds(r.T - HALO, HALO)
+        rows = pl.ds(part * (r.T // 2), r.T // 2)
         return line_copy(r, i, r.xg.at[slot, rows], r.xg.at[slot, rows], b.xg, slot, part)
 
-    x_adj(0, r.T - HALO)
+    x_adj(0, r.T // 2)
     for i in range(1, r.nY):
         start(r, x_copy(i, r.y, 0))
+    for part in range(2):
+        for i in range(1, r.nY):
+            relay_copy(r, i, lax.rem(r.y + i, r.nY), 1 - r.k, part).wait_recv()
+    grad_part(r, 0)
     u = r.u[...]
     r.di_p[...] = contract_first(low_adj, u).astype(BF16).reshape(2, r.nY, r.R // r.nS, r.C)
     start(r, pair_copy(r, r.di_p.at[1 - r.k], r.di_b, b.d5))
@@ -518,37 +565,21 @@
     weight_line(r, r.dt_c, r.dt_d, r.dt_e, (b.d2, b.d3))
 
     pl.when(r.s < r.nS - 1)(lambda: head_copy(r.s + 1).wait_recv())
-    x_adj(r.T - HALO, HALO)
+    x_adj(r.T // 2, r.T // 2)
     for i in range(1, r.nY):
         start(r, x_copy(i, r.y, 1))
-
-    for i in range(r.nY):
+    grad_part(r, 1)
+    weight_pair(r, r.di_p, r.di_b, r.di_c, (b.d5,))
+    spread(r, r.di_c, r.di_d, b.d6)
+    pair_copy(r, r.mi_p.at[1 - r.k], r.mi_b, b.m1).wait_recv()
+    r.mi_c[r.y] = (r.mi_p[r.k].astype(F32) + r.mi_b[...].astype(F32)).astype(BF16)
+    for i in range(1, r.nY):
+        start(r, line_copy(r, i, r.mi_c.at[r.y], r.mi_c.at[r.y], b.m2, r.y))
+    weight_back(r, r.dt_e, b.d3, b.d4)
+    for i in range(1, r.nY):
         y2 = lax.rem(r.y + i, r.nY)
-        if i:
-            x_copy(i, y2, 0).wait_recv()
-            x_copy(i, y2, 1).wait_recv()
-        for j in range(r.nX):
-            x2 = lax.rem(r.x + j, r.nX)
-            n = i * r.nX + j
-            r.hs[n] = contract_last(r.xg[y2], r.wp[x2]).astype(BF16)
-            if n == 0:
-
-                @pl.when(r.y == r.z)
-                def _():
-                    r.hr[r.c] = r.hs[0]
-
-                start(r, grad_copy(r, 0, 0), r.y != r.z)
-            else:
-                start(r, grad_copy(r, i, j))
-        if i == 0:
-            weight_pair(r, r.di_p, r.di_b, r.di_c, (b.d5,))
-            spread(r, r.di_c, r.di_d, b.d6)
-            pair_copy(r, r.mi_p.at[1 - r.k], r.mi_b, b.m1).wait_recv()
-            r.mi_c[r.y] = (r.mi_p[r.k].astype(F32) + r.mi_b[...].astype(F32)).astype(BF16)
-            for i2 in range(1, r.nY):
-                start(r, line_copy(r, i2, r.mi_c.at[r.y], r.mi_c.at[r.y], b.m2, r.y))
-        if i == 1:
-            weight_back(r, r.dt_e, b.d3, b.d4)
+        x_copy(i, y2, 0).wait_recv()
+        x_copy(i, y2, 1).wait_recv()
 
     x_all = r.xg[...].reshape(r.nY * r.T, r.C)
 
@@ -573,18 +604,13 @@
     weight_back(r, r.di_e, b.d7, b.d8)
     weight_end(r, r.dt_e, b.d4)
     pair_copy(r, r.mi_e.at[r.k], r.mi_e.at[1 - r.k], b.m3).wait_recv()
-    total = None
-    for j in range(r.nC):
-        c2 = lax.rem(r.c + j, r.nC)
-        wait = rcopy(
-            r.hs.at[0], r.hr.at[c2], r.sems[b.hg_s].at[0], r.sems[b.hg_r].at[c2], r.z * 2 + r.k, c2
-        )
-        if j == 0:
-            pl.when(r.y != r.z)(lambda wait=wait: wait.wait_recv())
-        else:
-            wait.wait_recv()
-        term = r.hr[c2].astype(F32)
-        total = term if total is None else total + term
+    total = r.hs[0].astype(F32)
+    for i, c2, dev in peers(r, b.chan):
+        for part in range(2):
+            rows, at = pl.ds(part * (r.T // 2), r.T // 2), part * r.nC + c2
+            got = r.hr.at[c2, rows]
+            rcopy(got, got, r.sems[b.hg_s].at[i], r.sems[b.hg_r].at[at], *dev).wait_recv()
+        total = total + r.hr[c2].astype(F32)
     r.hidden_out[...] = total.astype(BF16)
     weight_end(r, r.di_e, b.d8)
     flush(r)
@@ -610,7 +636,7 @@
     wide_row = rows + LANES
     buffers = dict(
         hg=((d.nX, d.nY, t, d.DH), BF16),
-        wp=((d.nX, d.DH, c), BF16),
+        wf=((d.nY, d.nX, d.DH, c), BF16),
         xs=((d.nY, t, c), BF16),
         xr=((d.nY, t, c), BF16),
         xt=((d.nY, HALO, c), BF16),
@@ -681,52 +707,61 @@
         w_dt_grad=((rows, c), F32),
         a_log_grad=((n, c), F32),
     )
-    sems = dict(loc=1)
+    sems = dict(loc=2, inp=12)
     pairs = (b.tu, b.wp, b.head, b.wg, b.d1, b.d4, b.d5, b.d8, b.m1, b.m3)
     lines = (b.xr, b.tail, b.d2, b.d3, b.d6, b.d7, b.m2)
     for key in pairs:
         sems[key + "_s"] = sems[key + "_r"] = 1
     for key in lines:
         sems[key + "_s"] = sems[key + "_r"] = d.nY
-    sems[b.xg_s] = sems[b.xg_r] = 2 * d.nY
+    for key in (b.xg, b.wy, b.wz):
+        sems[key + "_s"] = sems[key + "_r"] = 2 * d.nY
+    sems[b.hg_s] = sems[b.hg_r] = 2 * d.nC
     for key in (b.g1, b.g2):
         sems[key + "_s"] = sems[key + "_r"] = d.nX + d.nY
-    for key in (b.hg, b.p1, b.p2, b.p3, b.p4):
+    for key in (b.p1, b.p2, b.p3, b.p4):
         sems[key + "_s"] = sems[key + "_r"] = d.nC
     for key in (b.st, b.sd):
         sems[key + "_s"] = sems[key + "_r"] = d.nS
     return buffers, sems
 
 
-def run(dim, phases, groups, values, ins, outs, scratch, sem_names, number, cost):
+def run(dim, phases, remote, values, ins, outs, scratch, sem_names, cost):
     buffers, sem_sizes = tables(dim)
+    held = [name for name in ins if name not in (b.hidden, b.w_in)] if remote else []
 
     def body(*refs):
         r = types.SimpleNamespace(**dim)
-        for name, ref in zip(ins + outs + scratch, refs):
+        r.sent = []
+        names = ins + outs + scratch
+        for name, ref in zip(names, refs):
             setattr(r, name, ref)
-        r.sems = dict(zip(sem_names, refs[len(ins) + len(outs) + len(scratch) :]))
-        r.sent = []
-        if groups:
+        refs = refs[len(names) :]
+        r.sems = dict(zip(sem_names, refs))
+        if remote:
+            r.given = {name: getattr(r, name) for name in ins}
+            for name, ref in zip(held, refs[len(sem_names) :]):
+                setattr(r, name, ref)
             r.s, r.c = lax.axis_index(b.seq), lax.axis_index(b.chan)
             r.y, r.k = lax.div(r.s, 2), lax.rem(r.s, 2)
             r.z, r.x = lax.div(r.c, r.nX), lax.rem(r.c, r.nX)
-            greet(r, groups)
+            greet(r, functools.partial(load, r))
         for phase in phases:
             phase(r)
 
     space = pl.BlockSpec(memory_space=pltpu.VMEM)
-    extra = dict(collective_id=number, has_side_effects=True) if groups else {}
+    extra = dict(collective_id=0, has_side_effects=True) if remote else {}
     results = pl.pallas_call(
         body,
         out_shape=[jax.ShapeDtypeStruct(*buffers[name]) for name in outs],
-        in_specs=[space] * len(ins),
+        in_specs=[pl.BlockSpec(memory_space=pl.ANY) if remote else space] * len(ins),
         out_specs=[space] * len(outs),
         scratch_shapes=[pltpu.VMEM(*buffers[name]) for name in scratch]
-        + [pltpu.SemaphoreType.DMA((sem_sizes[name],)) for name in sem_names],
+        + [pltpu.SemaphoreType.DMA((sem_sizes[name],)) for name in sem_names]
+        + [pltpu.VMEM(values[name].shape, values[name].dtype) for name in held],
         compiler_params=pltpu.CompilerParams(vmem_limit_bytes=56 << 20, **extra),
         cost_estimate=pl.CostEstimate(flops=cost, bytes_accessed=4 << 20, transcendentals=0),
-        name=phases[0].__name__,
+        name=phases[-1].__name__,
     )(*[values[name] for name in ins])
     values.update(zip(outs, results))
 
@@ -769,8 +804,9 @@
     given = list(v)
     buffers, sems = tables(dim)
     scratch = [name for name in buffers if name not in given + raw + ORDER]
-    run(dim, [take_hidden, project, prepare, scan, gradients], [b.cross, b.chan, b.seq], v, given, raw, scratch, list(sems), 0, 2_000_000_000)
-    run(dim, [finish], [], v, raw, ORDER, [], [], 0, 1_000_000)
+    phases = [take_hidden, project, prepare, scan, gradients]
+    run(dim, phases, True, v, given, raw, scratch, list(sems), 2_000_000_000)
+    run(dim, [finish], False, v, raw, ORDER, [], [], 1_000_000)
     v[b.w_in_grad] = v[b.w_in_grad].reshape(w_in.shape)
     return tuple(v[name] for name in ORDER)
 

time: 103 us -> 94 us (0.913)
  Pallas kernels: 102 us -> 93.2 us
    pallas_call x2, Pallas kernels: 102 us -> 93.2 us  [run(): pl.pallas_call(body, out_shape=[jax.ShapeDtypeStruct(*buffers[name]) for...]
where the time goes in v3:
time: 94 us; the launch traced here: 93.9 us
  Pallas kernels  93.2 us (99%)
    pallas_call x2, Pallas kernels, run(): pl.pallas_call(body, out_shape=[jax.ShapeDtypeStruct(*buffers[name]) for...  93.2 us

profile of v3, /device:TPU:1, one launch (start us, length us, event | category | flops | bytes accessed | tf_op | source)
XLA Modules:
  0.0 93.9 jit_solution(10088829124329983901)
XLA Ops:
  0.6 90.5 %gradients.1 = (bf16[128,256]{1,0:T(8,128)(2,1)}, bf16[128,512]{1,0:T(8,128)(2,1)}, bf16[2,256,512]{2,1,0:T(8,128)(2,1)}, bf16[2,4,32,512]{3,2,1,0:T(8,128)(2,1)...) custom-call(bf16[128,256]{1,0:T(8,128)(2,1)} %refs_0_.1, bf16[128,512]{1,0:T(8,128)(2,1)} %refs_1_.1, ...), custom_call_target="tpu_custom_call" | custom-call | flops 2000000000 | bytes 4194304 | tf_op jit(solution)/shard_map/gradients/pallas_call | solution.py:754
  91.1 2.7 %finish.1 = (bf16[128,256]{1,0:T(8,128)(2,1)}, bf16[128,512]{1,0:T(8,128)(2,1)}, f32[2,256,512]{2,1,0:T(8,128)}, f32[256,512]{1,0:T(8,128)}, f32[32,512]{1,0:T(8...) custom-call(bf16[128,256]{1,0:T(8,128)(2,1)} %get-tuple-element.20.refs_0_, bf16[128,512]{1,0:T(8,128)(2,1)} %get-tuple-element.21.refs_1_, ...), custom_call_target="tpu_custom_call" | custom-call | flops 1000000 | bytes 4194304 | tf_op jit(solution)/shard_map/finish/pallas_call | solution.py:754

commit v4 on v3

--- a/solution.py
+++ b/solution.py
@@ -339,66 +339,99 @@
         r.cx[t] = jnp.broadcast_to(turned[r.N : 2 * r.N, t : t + 1], (r.N, LANES))
 
 
-def forward(r, init, full):
+def forward_chunk(r, j, h, kept):
     a_mat = r.am[...]
-    if full:
-        mask = block_mask(r, CH)
-        r.hh[pl.ds(0, r.N), :] = init
-
-    def chunk(j, h):
-        base = pl.multiple_of(j * CH, CH)
-        d = r.delta[pl.ds(base, CH), :]
-        du = r.du[pl.ds(base, CH), :]
-        kept = []
-        for t in range(CH):
-            at = pl.multiple_of((base + t) * r.N, r.N)
-            if full:
-                a = r.aa[pl.ds(at, r.N), :]
-            else:
-                a = jnp.exp(d[t : t + 1, :] * a_mat)
-                r.aa[pl.ds(at, r.N), :] = a
-            h = a * h + du[t : t + 1, :] * wide(r, r.bx[base + t])
-            if full:
-                r.hh[pl.ds(at + r.N, r.N), :] = h
-                kept.append(h.astype(BF16))
-        if full:
-            rows = jnp.concatenate(kept, 0)
-            r.y_scan[pl.ds(base, CH), :] = dot(r.cd[pl.ds(base, CH), :], rows)
-            r.cm[pl.ds(base, CH), :] = mask * contract_last(r.g[pl.ds(base, CH), :].astype(BF16), rows)
-        return h
-
-    return lax.fori_loop(0, r.T // CH, chunk, init)
-
-
-def backward(r, init, full):
+    base = pl.multiple_of(j * CH, CH)
+    d = r.delta[pl.ds(base, CH), :]
+    du = r.du[pl.ds(base, CH), :]
+    for t in range(CH):
+        at = pl.multiple_of((base + t) * r.N, r.N)
+        if kept is None:
+            a = jnp.exp(d[t : t + 1, :] * a_mat)
+            r.aa[pl.ds(at, r.N), :] = a
+        else:
+            a = r.aa[pl.ds(at, r.N), :]
+        h = a * h + du[t : t + 1, :] * wide(r, r.bx[base + t])
+        if kept is not None:
+            r.hh[pl.ds(at + r.N, r.N), :] = h
+            kept[pl.ds(t * r.N, r.N), :] = h.astype(BF16)
+    return h
+
+
+def forward_sums(r, j, kept, mask):
+    rows = pl.ds(pl.multiple_of(j * CH, CH), CH)
+    states = kept[...]
+    r.y_scan[rows, :] = dot(r.cd[rows, :], states)
+    r.cm[rows, :] = mask * contract_last(r.g[rows, :].astype(BF16), states)
+
+
+def forward_free(r):
+    return lax.fori_loop(0, r.T // CH, lambda j, h: forward_chunk(r, j, h, None), jnp.zeros((r.N, r.C), F32))
+
+
+def forward_full(r):
+    mask = block_mask(r, CH)
+    r.hh[pl.ds(0, r.N), :] = r.h_in[...]
+    r.kept1[...] = jnp.zeros_like(r.kept1)
+
+    def two(i, h):
+        forward_sums(r, jnp.maximum(2 * i - 1, 0), r.kept1, mask)
+        h = forward_chunk(r, 2 * i, h, r.kept0)
+        forward_sums(r, 2 * i, r.kept0, mask)
+        return forward_chunk(r, 2 * i + 1, h, r.kept1)
+
+    lax.fori_loop(0, r.T // CH // 2, two, r.h_in[...])
+    forward_sums(r, r.T // CH - 1, r.kept1, mask)
+
+
+def backward_chunk(r, j, carry, kept):
     a_mat = r.am[...]
+    base = pl.multiple_of(j * CH, CH)
+    kap, acc = carry
+    d = r.delta[pl.ds(base, CH), :]
+    g = r.g[pl.ds(base, CH), :]
+    for t in reversed(range(CH)):
+        at = pl.multiple_of((base + t) * r.N, r.N)
+        lam = kap + wide(r, r.cx[base + t]) * g[t : t + 1, :]
+        kap = r.aa[pl.ds(at, r.N), :] * lam
+        if kept is not None:
+            q = kap * r.hh[pl.ds(at, r.N), :]
+            acc = acc + q * d[t : t + 1, :]
+            kept[0][pl.ds(t * r.N, r.N), :] = lam.astype(BF16)
+            kept[1][pl.ds(t * r.N, r.N), :] = (q * a_mat).astype(BF16)
+    return kap, acc
+
+
+def backward_sums(r, j, kept, mask):
+    rows = pl.ds(pl.multiple_of(j * CH, CH), CH)
+    lam = kept[0][...]
+    r.s1[rows, :] = dot(r.bd[rows, :], lam)
+    r.s2[rows, :] = dot(mask.astype(BF16), kept[1][...])
+    r.bm[rows, :] = mask * contract_last(r.du[rows, :].astype(BF16), lam)
+
+
+def backward_free(r):
+    zero = jnp.zeros((r.N, r.C), F32)
+    last = r.T // CH - 1
+    return lax.fori_loop(0, last + 1, lambda i, c: backward_chunk(r, last - i, c, None), (zero, zero))[0]
+
+
+def backward_full(r):
     mask = block_mask(r, CH)
-    chunks = r.T // CH
-
-    def chunk(i, carry):
-        base = pl.multiple_of((chunks - 1 - i) * CH, CH)
-        kap, acc = carry
-        d = r.delta[pl.ds(base, CH), :]
-        g = r.g[pl.ds(base, CH), :]
-        lams, qas = [None] * CH, [None] * CH
-        for t in reversed(range(CH)):
-            at = pl.multiple_of((base + t) * r.N, r.N)
-            lam = kap + wide(r, r.cx[base + t]) * g[t : t + 1, :]
-            kap = r.aa[pl.ds(at, r.N), :] * lam
-            if full:
-                q = kap * r.hh[pl.ds(at, r.N), :]
-                acc = acc + q * d[t : t + 1, :]
-                qas[t] = (q * a_mat).astype(BF16)
-                lams[t] = lam.astype(BF16)
-        if full:
-            lam_rows = jnp.concatenate(lams, 0)
-            du = r.du[pl.ds(base, CH), :]
-            r.s1[pl.ds(base, CH), :] = dot(r.bd[pl.ds(base, CH), :], lam_rows)
-            r.s2[pl.ds(base, CH), :] = dot(mask.astype(BF16), jnp.concatenate(qas, 0))
-            r.bm[pl.ds(base, CH), :] = mask * contract_last(du.astype(BF16), lam_rows)
-        return kap, acc
-
-    return lax.fori_loop(0, chunks, chunk, (init, jnp.zeros_like(init)))
+    last = r.T // CH - 1
+    even, odd = (r.kept0, r.kept2), (r.kept1, r.kept3)
+    for ref in odd:
+        ref[...] = jnp.zeros_like(ref)
+
+    def two(i, carry):
+        backward_sums(r, jnp.minimum(last - 2 * i + 1, last), odd, mask)
+        carry = backward_chunk(r, last - 2 * i, carry, even)
+        backward_sums(r, last - 2 * i, even, mask)
+        return backward_chunk(r, last - 2 * i - 1, carry, odd)
+
+    a_adj = lax.fori_loop(0, r.T // CH // 2, two, (r.l_in[...], jnp.zeros((r.N, r.C), F32)))[1]
+    backward_sums(r, 0, odd, mask)
+    return a_adj
 
 
 def state_copy(r, which, j, slot):
@@ -407,10 +440,10 @@
 
 def scan(r):
     zero = jnp.zeros((r.N, r.C), F32)
-    r.ef[0] = forward(r, zero, False).astype(BF16)
+    r.ef[0] = forward_free(r).astype(BF16)
     for j in range(1, r.nS):
         start(r, state_copy(r, 0, j, r.s), j > r.s)
-    r.ef[1] = backward(r, zero, False)[0].astype(BF16)
+    r.ef[1] = backward_free(r).astype(BF16)
     for j in range(r.nS - 1):
         start(r, state_copy(r, 1, j, r.s), j < r.s)
     picked = pick(r)
@@ -426,11 +459,14 @@
     r.h_in[...] = zero
     for j in range(r.nS - 1):
         pl.when(j < r.s)(functools.partial(enter, j, r.h_in))
-    forward(r, r.h_in[...], True)
+    forward_full(r)
     r.l_in[...] = zero
     for j in range(r.nS - 1, 0, -1):
         pl.when(j > r.s)(functools.partial(enter, j, r.l_in))
-    a_adj = backward(r, r.l_in[...], True)[1]
+    r.ug[r.y] = r.u[...]
+    for i in range(1, r.nY):
+        start(r, line_copy(r, i, r.ug.at[r.y], r.ug.at[r.y], b.ug, r.y))
+    a_adj = backward_full(r)
     s1 = r.s1[...]
     u = r.u[...].astype(F32)
     pre_adj = ((u * s1 + r.s2[...]) * jax.nn.sigmoid(r.pre[...])).astype(BF16)
@@ -448,7 +484,8 @@
     alog = (a_adj * r.am[...]).astype(BF16)
     wide_half = r.C // 2
     for j in range(2):
-        r.mi_p[j, pl.ds(2 * r.N, r.N), :] = alog[:, j * wide_half : (j + 1) * wide_half]
+        r.mi_p[j] = alog[:, j * wide_half : (j + 1) * wide_half]
+    start(r, pair_copy(r, r.mi_p.at[1 - r.k], r.mi_b, b.m1))
     skip = r.skip_d[...]
     r.uu[...] = r.delta[...] * s1 + skip * r.g[...]
     r.gate_out[...] = (r.gs[...] * (r.y_scan[...] + skip * u)).astype(BF16)
@@ -513,8 +550,15 @@
     gather_start(r, b.chan, r.part2_a, b.p4)
     weight_pair(r, r.dt_p, r.dt_b, r.dt_c, (b.d1,))
     spread(r, r.dt_c, r.dt_d, b.d2)
+    pair_copy(r, r.mi_p.at[1 - r.k], r.mi_b, b.m1).wait_recv()
+    r.mi_c[r.y] = (r.mi_p[r.k].astype(F32) + r.mi_b[...].astype(F32)).astype(BF16)
+    for i in range(1, r.nY):
+        start(r, line_copy(r, i, r.mi_c.at[r.y], r.mi_c.at[r.y], b.m2, r.y))
     recv_wait(r, b.chan, r.part2_a, b.p4)
     full = r.part2_a[...].reshape(r.T, r.R + LANES)
+    r.lg[r.y] = full.astype(BF16)
+    for i in range(1, r.nY):
+        start(r, line_copy(r, i, r.lg.at[r.y], r.lg.at[r.y], b.lg, r.y))
     low_adj = full[:, : r.R].astype(BF16)
     bc_adj = full[:, r.R : r.R + 2 * r.N].astype(BF16)
     u_adj = r.uu[...] + dot(low_adj, r.w_delta_in[...]) + dot(bc_adj, r.w_bc[...])
@@ -555,27 +599,30 @@
         for i in range(1, r.nY):
             relay_copy(r, i, lax.rem(r.y + i, r.nY), 1 - r.k, part).wait_recv()
     grad_part(r, 0)
-    u = r.u[...]
-    r.di_p[...] = contract_first(low_adj, u).astype(BF16).reshape(2, r.nY, r.R // r.nS, r.C)
-    start(r, pair_copy(r, r.di_p.at[1 - r.k], r.di_b, b.d5))
-    bc_term = contract_first(bc_adj, u).astype(BF16)
-    for j in range(2):
-        r.mi_p[j, pl.ds(0, 2 * r.N), :] = bc_term[:, j * wide_half : (j + 1) * wide_half]
-    start(r, pair_copy(r, r.mi_p.at[1 - r.k], r.mi_b, b.m1))
     weight_line(r, r.dt_c, r.dt_d, r.dt_e, (b.d2, b.d3))
-
     pl.when(r.s < r.nS - 1)(lambda: head_copy(r.s + 1).wait_recv())
     x_adj(r.T // 2, r.T // 2)
     for i in range(1, r.nY):
         start(r, x_copy(i, r.y, 1))
     grad_part(r, 1)
-    weight_pair(r, r.di_p, r.di_b, r.di_c, (b.d5,))
-    spread(r, r.di_c, r.di_d, b.d6)
-    pair_copy(r, r.mi_p.at[1 - r.k], r.mi_b, b.m1).wait_recv()
-    r.mi_c[r.y] = (r.mi_p[r.k].astype(F32) + r.mi_b[...].astype(F32)).astype(BF16)
-    for i in range(1, r.nY):
-        start(r, line_copy(r, i, r.mi_c.at[r.y], r.mi_c.at[r.y], b.m2, r.y))
+    total = None
+    for y2 in range(r.nY):
+        pl.when(r.y != y2)(
+            line_copy(r, 1, r.mi_c.at[y2], r.mi_c.at[y2], b.m2, y2).wait_recv
+        )
+        term = r.mi_c[y2].astype(F32)
+        total = term if total is None else total + term
+    r.mi_e[r.k] = total
+    start(r, pair_copy(r, r.mi_e.at[r.k], r.mi_e.at[r.k], b.m3))
     weight_back(r, r.dt_e, b.d3, b.d4)
+    for i in range(1, r.nY):
+        y2 = lax.rem(r.y + i, r.nY)
+        line_copy(r, i, r.ug.at[y2], r.ug.at[y2], b.ug, y2).wait_recv()
+        line_copy(r, i, r.lg.at[y2], r.lg.at[y2], b.lg, y2).wait_recv()
+    tokens = r.nY * r.T
+    term = contract_first(r.lg[...].reshape(tokens, r.R + LANES), r.ug[...].reshape(tokens, r.C))
+    r.li_p[...] = term[: r.R + 2 * r.N].astype(BF16)
+    start(r, pair_copy(r, r.li_p, r.li_b, b.d5))
     for i in range(1, r.nY):
         y2 = lax.rem(r.y + i, r.nY)
         x_copy(i, y2, 0).wait_recv()
@@ -589,19 +636,10 @@
     for j in range(half):
         r.ws[j] = weight((1 - r.k) * half + j).astype(BF16)
     start(r, pair_copy(r, r.ws, r.wr, b.wg))
-    weight_line(r, r.di_c, r.di_d, r.di_e, (b.d6, b.d7))
-    total = r.mi_c[r.y].astype(F32)
-    for i in range(1, r.nY):
-        y2 = lax.rem(r.y + i, r.nY)
-        line_copy(r, i, r.mi_c.at[y2], r.mi_c.at[y2], b.m2, y2).wait_recv()
-        total = total + r.mi_c[y2].astype(F32)
-    r.mi_e[r.k] = total
-    start(r, pair_copy(r, r.mi_e.at[r.k], r.mi_e.at[r.k], b.m3))
     for j in range(half):
         r.wo[j] = weight(r.k * half + j)
     pair_copy(r, r.ws, r.wr, b.wg).wait_recv()
     r.w_out[...] = (r.wo[...] + r.wr[...].astype(F32)).astype(BF16)
-    weight_back(r, r.di_e, b.d7, b.d8)
     weight_end(r, r.dt_e, b.d4)
     pair_copy(r, r.mi_e.at[r.k], r.mi_e.at[1 - r.k], b.m3).wait_recv()
     total = r.hs[0].astype(F32)
@@ -612,7 +650,8 @@
             rcopy(got, got, r.sems[b.hg_s].at[i], r.sems[b.hg_r].at[at], *dev).wait_recv()
         total = total + r.hr[c2].astype(F32)
     r.hidden_out[...] = total.astype(BF16)
-    weight_end(r, r.di_e, b.d8)
+    pair_copy(r, r.li_p, r.li_b, b.d5).wait_recv()
+    r.li_e[...] = r.li_p[...].astype(F32) + r.li_b[...].astype(F32)
     flush(r)
 
 
@@ -623,11 +662,11 @@
     r.gate_grad[...] = r.gate_out[...]
     r.w_in_grad[...] = r.w_out[...].astype(F32) * scale
     r.w_dt_grad[...] = r.dt_e[...].astype(F32).reshape(r.R, r.C) * scale
-    r.w_delta_in_grad[...] = r.di_e[...].astype(F32).reshape(r.R, r.C) * scale
+    r.w_delta_in_grad[...] = r.li_e[pl.ds(0, r.R), :] * scale
+    r.w_bc_grad[...] = r.li_e[pl.ds(r.R, 2 * r.N), :] * scale
     for j in range(2):
         cols = pl.ds(j * wide_half, wide_half)
-        r.w_bc_grad[:, cols] = r.mi_e[j, pl.ds(0, 2 * r.N), :] * scale
-        r.a_log_grad[:, cols] = r.mi_e[j, pl.ds(2 * r.N, r.N), :] * scale
+        r.a_log_grad[:, cols] = r.mi_e[j] * scale
 
 
 def tables(dim):
@@ -662,6 +701,10 @@
         ef=((2, n, c), BF16),
         st_r=((d.nS, n, c), BF16),
         sd_r=((d.nS, 1, c), F32),
+        kept0=((CH * n, c), BF16),
+        kept1=((CH * n, c), BF16),
+        kept2=((CH * n, c), BF16),
+        kept3=((CH * n, c), BF16),
         h_in=((n, c), F32),
         l_in=((n, c), F32),
         bd=((t, CH * n), BF16),
@@ -680,15 +723,15 @@
         dt_c=((d.nY, q, c), BF16),
         dt_d=((d.nY, q, c), BF16),
         dt_e=((2, d.nY, q, c), BF16),
-        di_p=((2, d.nY, q, c), BF16),
-        di_b=((d.nY, q, c), BF16),
-        di_c=((d.nY, q, c), BF16),
-        di_d=((d.nY, q, c), BF16),
-        di_e=((2, d.nY, q, c), BF16),
-        mi_p=((2, 3 * n, c // 2), BF16),
-        mi_b=((3 * n, c // 2), BF16),
-        mi_c=((d.nY, 3 * n, c // 2), BF16),
-        mi_e=((2, 3 * n, c // 2), F32),
+        ug=((d.nY, t, c), BF16),
+        lg=((d.nY, t, wide_row), BF16),
+        li_p=((rows + 2 * n, c), BF16),
+        li_b=((rows + 2 * n, c), BF16),
+        li_e=((rows + 2 * n, c), F32),
+        mi_p=((2, n, c // 2), BF16),
+        mi_b=((n, c // 2), BF16),
+        mi_c=((d.nY, n, c // 2), BF16),
+        mi_e=((2, n, c // 2), F32),
         cpad=((t + HEAD, c), F32),
         xg=((d.nY, t, c), BF16),
         hs=((d.nC, t, d.DH), BF16),
@@ -708,8 +751,8 @@
         a_log_grad=((n, c), F32),
     )
     sems = dict(loc=2, inp=12)
-    pairs = (b.tu, b.wp, b.head, b.wg, b.d1, b.d4, b.d5, b.d8, b.m1, b.m3)
-    lines = (b.xr, b.tail, b.d2, b.d3, b.d6, b.d7, b.m2)
+    pairs = (b.tu, b.wp, b.head, b.wg, b.d1, b.d4, b.d5, b.m1, b.m3)
+    lines = (b.xr, b.tail, b.d2, b.d3, b.m2, b.ug, b.lg)
     for key in pairs:
         sems[key + "_s"] = sems[key + "_r"] = 1
     for key in lines:
@@ -800,7 +843,7 @@
         a_log=a_log,
         skip_d=skip_d[None],
     )
-    raw = [b.hidden_out, b.gate_out, b.w_out, b.dt_e, b.di_e, b.mi_e]
+    raw = [b.hidden_out, b.gate_out, b.w_out, b.dt_e, b.li_e, b.mi_e]
     given = list(v)
     buffers, sems = tables(dim)
     scratch = [name for name in buffers if name not in given + raw + ORDER]

time: 94 us -> 91.8 us (0.977)
  Pallas kernels: 93.2 us -> 91 us
    pallas_call x2, Pallas kernels: 93.2 us -> 91 us  [run(): pl.pallas_call(body, out_shape=[jax.ShapeDtypeStruct(*buffers[name]) for...]
where the time goes in v4:
time: 91.8 us; the launch traced here: 91.7 us
  Pallas kernels  91 us (99%)
    pallas_call x2, Pallas kernels, run(): pl.pallas_call(body, out_shape=[jax.ShapeDtypeStruct(*buffers[name]) for...  91 us

profile of v4, /device:TPU:1, one launch (start us, length us, event | category | flops | bytes accessed | tf_op | source)
XLA Modules:
  0.0 91.7 jit_solution(2835697677890543101)
XLA Ops:
  0.6 88.2 %gradients.1 = (bf16[128,256]{1,0:T(8,128)(2,1)}, bf16[128,512]{1,0:T(8,128)(2,1)}, bf16[2,256,512]{2,1,0:T(8,128)(2,1)}, bf16[2,4,32,512]{3,2,1,0:T(8,128)(2,1)...) custom-call(bf16[128,256]{1,0:T(8,128)(2,1)} %refs_0_.1, bf16[128,512]{1,0:T(8,128)(2,1)} %refs_1_.1, ...), custom_call_target="tpu_custom_call" | custom-call | flops 2000000000 | bytes 4194304 | tf_op jit(solution)/shard_map/gradients/pallas_call | solution.py:797
  88.8 2.8 %finish.1 = (bf16[128,256]{1,0:T(8,128)(2,1)}, bf16[128,512]{1,0:T(8,128)(2,1)}, f32[2,256,512]{2,1,0:T(8,128)}, f32[256,512]{1,0:T(8,128)}, f32[32,512]{1,0:T(8...) custom-call(bf16[128,256]{1,0:T(8,128)(2,1)} %get-tuple-element.20.refs_0_, bf16[128,512]{1,0:T(8,128)(2,1)} %get-tuple-element.21.refs_1_, ...), custom_call_target="tpu_custom_call" | custom-call | flops 1000000 | bytes 4194304 | tf_op jit(solution)/shard_map/finish/pallas_call | solution.py:797

commit v5 on v4

--- a/solution.py
+++ b/solution.py
@@ -164,6 +164,21 @@
     for name in names:
         at = list(r.given).index(name)
         pltpu.make_async_copy(r.given[name], getattr(r, name), r.sems[b.inp].at[at]).wait()
+
+
+def pack(r, low, small):
+    r.pad[:, pl.ds(0, 2 * r.N)] = small
+    parts = [low[:, at : at + LANES] for at in range(0, r.R, LANES)] + [r.pad[...]]
+    parts = [part.reshape(r.nC, r.RP, LANES) for part in parts]
+    parts += [jnp.zeros_like(parts[0])] * (r.PR // r.RP - len(parts))
+    return jnp.concatenate(parts, 1).astype(BF16)
+
+
+def unpack(r, pieces):
+    pieces = pieces.astype(F32)
+    parts = [pieces[:, at : at + r.RP].reshape(r.T, LANES) for at in range(0, r.PR, r.RP)]
+    count = r.R // LANES
+    return jnp.concatenate(parts[:count], 1), parts[count]
 
 
 def weight_rows(r, y2, core, part):
@@ -213,8 +228,7 @@
     r.g[...] = grad * (gate * sig)
     r.gs[...] = grad * (sig * (1.0 + gate * (1.0 - sig)))
     r.am[...] = -jnp.exp(r.a_log[...])
-    r.part[:, :, pl.ds(r.R, LANES)] = jnp.zeros((r.nC, r.RP, LANES), F32)
-    r.part2[:, :, pl.ds(r.R, LANES)] = jnp.zeros((r.nC, r.RP, LANES), F32)
+    r.pad[...] = jnp.zeros_like(r.pad)
     own_w.wait()
     pl.when(r.y == r.z)(own_h.wait)
 
@@ -292,18 +306,16 @@
     sig = jax.nn.sigmoid(conv)
     u = (conv * sig).astype(BF16)
     r.u[...] = u
-    r.part[:, :, pl.ds(0, r.R)] = contract_last(u, r.w_delta_in[...]).reshape(r.nC, r.RP, r.R)
-    r.part[:, :, pl.ds(r.R, 2 * r.N)] = contract_last(u, r.w_bc[...]).reshape(r.nC, r.RP, 2 * r.N)
+    r.part[...] = pack(r, contract_last(u, r.w_delta_in[...]), contract_last(u, r.w_bc[...]))
     scatter_start(r, b.chan, r.part, r.part_r, b.p1)
     weight_send(r, 1)
     weight_relay(r, 0)
     r.slope[...] = sig * (1.0 + conv * (1.0 - sig))
-    r.part_a[r.c] = scatter_sum(r, b.chan, r.part, r.part_r, b.p1)
+    r.part_a[r.c] = scatter_sum(r, b.chan, r.part, r.part_r, b.p1).astype(BF16)
     gather_start(r, b.chan, r.part_a, b.p2)
     recv_wait(r, b.chan, r.part_a, b.p2)
-    full = r.part_a[...].reshape(r.T, r.R + LANES)
-    r.low[...] = full[:, : r.R].astype(BF16)
-    r.bcw[...] = full[:, r.R :]
+    low, r.bcw[...] = unpack(r, r.part_a[...])
+    r.low[...] = low.astype(BF16)
 
 
 def wide(r, b):
@@ -336,7 +348,6 @@
     turned = r.bcw[...].T
     for t in range(r.T):
         r.bx[t] = jnp.broadcast_to(turned[0 : r.N, t : t + 1], (r.N, LANES))
-        r.cx[t] = jnp.broadcast_to(turned[r.N : 2 * r.N, t : t + 1], (r.N, LANES))
 
 
 def forward_chunk(r, j, h, kept):
@@ -443,6 +454,9 @@
     r.ef[0] = forward_free(r).astype(BF16)
     for j in range(1, r.nS):
         start(r, state_copy(r, 0, j, r.s), j > r.s)
+    turned = r.bcw[...].T
+    for t in range(r.T):
+        r.cx[t] = jnp.broadcast_to(turned[r.N : 2 * r.N, t : t + 1], (r.N, LANES))
     r.ef[1] = backward_free(r).astype(BF16)
     for j in range(r.nS - 1):
         start(r, state_copy(r, 1, j, r.s), j < r.s)
@@ -474,9 +488,7 @@
     nt = (((1,), (1,)), ((), ()))
     b_adj = lax.dot_general(r.bm[...], picked, nt, precision=exact, preferred_element_type=F32)
     c_adj = lax.dot_general(r.cm[...], picked, nt, precision=exact, preferred_element_type=F32)
-    r.part2[:, :, pl.ds(0, r.R)] = contract_last(pre_adj, r.w_dt[...]).reshape(r.nC, r.RP, r.R)
-    r.part2[:, :, pl.ds(r.R, r.N)] = b_adj.reshape(r.nC, r.RP, r.N)
-    r.part2[:, :, pl.ds(r.R + r.N, r.N)] = c_adj.reshape(r.nC, r.RP, r.N)
+    r.part2[...] = pack(r, contract_last(pre_adj, r.w_dt[...]), jnp.concatenate([b_adj, c_adj], 1))
     scatter_start(r, b.chan, r.part2, r.part2_r, b.p3)
     weight_relay(r, 1)
     r.dt_p[...] = contract_first(r.low[...], pre_adj).astype(BF16).reshape(2, r.nY, r.R // r.nS, r.C)
@@ -546,7 +558,7 @@
     half = r.nX // 2
     wide_half = r.C // 2
     flush(r)
-    r.part2_a[r.c] = scatter_sum(r, b.chan, r.part2, r.part2_r, b.p3)
+    r.part2_a[r.c] = scatter_sum(r, b.chan, r.part2, r.part2_r, b.p3).astype(BF16)
     gather_start(r, b.chan, r.part2_a, b.p4)
     weight_pair(r, r.dt_p, r.dt_b, r.dt_c, (b.d1,))
     spread(r, r.dt_c, r.dt_d, b.d2)
@@ -555,12 +567,12 @@
     for i in range(1, r.nY):
         start(r, line_copy(r, i, r.mi_c.at[r.y], r.mi_c.at[r.y], b.m2, r.y))
     recv_wait(r, b.chan, r.part2_a, b.p4)
-    full = r.part2_a[...].reshape(r.T, r.R + LANES)
-    r.lg[r.y] = full.astype(BF16)
+    full = jnp.concatenate(unpack(r, r.part2_a[...]), 1).astype(BF16)
+    r.lg[r.y] = full
     for i in range(1, r.nY):
         start(r, line_copy(r, i, r.lg.at[r.y], r.lg.at[r.y], b.lg, r.y))
-    low_adj = full[:, : r.R].astype(BF16)
-    bc_adj = full[:, r.R : r.R + 2 * r.N].astype(BF16)
+    low_adj = full[:, : r.R]
+    bc_adj = full[:, r.R : r.R + 2 * r.N]
     u_adj = r.uu[...] + dot(low_adj, r.w_delta_in[...]) + dot(bc_adj, r.w_bc[...])
     conv_adj = u_adj * r.slope[...]
     r.cpad[pl.ds(0, r.T), :] = conv_adj
@@ -651,7 +663,7 @@
         total = total + r.hr[c2].astype(F32)
     r.hidden_out[...] = total.astype(BF16)
     pair_copy(r, r.li_p, r.li_b, b.d5).wait_recv()
-    r.li_e[...] = r.li_p[...].astype(F32) + r.li_b[...].astype(F32)
+    r.li_e[...] = (r.li_p[...].astype(F32) + r.li_b[...].astype(F32)).astype(BF16)
     flush(r)
 
 
@@ -662,8 +674,8 @@
     r.gate_grad[...] = r.gate_out[...]
     r.w_in_grad[...] = r.w_out[...].astype(F32) * scale
     r.w_dt_grad[...] = r.dt_e[...].astype(F32).reshape(r.R, r.C) * scale
-    r.w_delta_in_grad[...] = r.li_e[pl.ds(0, r.R), :] * scale
-    r.w_bc_grad[...] = r.li_e[pl.ds(r.R, 2 * r.N), :] * scale
+    r.w_delta_in_grad[...] = r.li_e[pl.ds(0, r.R), :].astype(F32) * scale
+    r.w_bc_grad[...] = r.li_e[pl.ds(r.R, 2 * r.N), :].astype(F32) * scale
     for j in range(2):
         cols = pl.ds(j * wide_half, wide_half)
         r.a_log_grad[:, cols] = r.mi_e[j] * scale
@@ -683,9 +695,10 @@
         slope=((t, c), F32),
         gs=((t, c), F32),
         u=((t, c), BF16),
-        part=((d.nC, d.RP, wide_row), F32),
-        part_r=((d.nC, d.RP, wide_row), F32),
-        part_a=((d.nC, d.RP, wide_row), F32),
+        part=((d.nC, d.PR, LANES), BF16),
+        part_r=((d.nC, d.PR, LANES), BF16),
+        part_a=((d.nC, d.PR, LANES), BF16),
+        pad=((t, LANES), F32),
         low=((t, rows), BF16),
         bcw=((t, LANES), F32),
         pre=((t, c), F32),
@@ -715,9 +728,9 @@
         s1=((t, c), F32),
         s2=((t, c), F32),
         uu=((t, c), F32),
-        part2=((d.nC, d.RP, wide_row), F32),
-        part2_r=((d.nC, d.RP, wide_row), F32),
-        part2_a=((d.nC, d.RP, wide_row), F32),
+        part2=((d.nC, d.PR, LANES), BF16),
+        part2_r=((d.nC, d.PR, LANES), BF16),
+        part2_a=((d.nC, d.PR, LANES), BF16),
         dt_p=((2, d.nY, q, c), BF16),
         dt_b=((d.nY, q, c), BF16),
         dt_c=((d.nY, q, c), BF16),
@@ -727,7 +740,7 @@
         lg=((d.nY, t, wide_row), BF16),
         li_p=((rows + 2 * n, c), BF16),
         li_b=((rows + 2 * n, c), BF16),
-        li_e=((rows + 2 * n, c), F32),
+        li_e=((rows + 2 * n, c), BF16),
         mi_p=((2, n, c // 2), BF16),
         mi_b=((n, c // 2), BF16),
         mi_c=((d.nY, n, c // 2), BF16),
@@ -828,6 +841,7 @@
         N=a_log.shape[0],
         KC=conv_w.shape[0],
         RP=hidden.shape[0] // chan,
+        PR=-(-(hidden.shape[0] // chan) * (w_delta_in.shape[0] // LANES + 1) // 16) * 16,
     )
     v = dict(
         hidden=hidden,

time: 91.8 us -> 90.1 us (0.981)
  Pallas kernels: 91 us -> 89.3 us
    pallas_call x2, Pallas kernels: 91 us -> 89.3 us  [run(): pl.pallas_call(body, out_shape=[jax.ShapeDtypeStruct(*buffers[name]) for...]
where the time goes in v5:
time: 90.1 us; the launch traced here: 89.9 us
  Pallas kernels  89.3 us (99%)
    pallas_call x2, Pallas kernels, run(): pl.pallas_call(body, out_shape=[jax.ShapeDtypeStruct(*buffers[name]) for...  89.3 us

profile of v5, /device:TPU:1, one launch (start us, length us, event | category | flops | bytes accessed | tf_op | source)
XLA Modules:
  0.0 89.9 jit_solution(8664648671429195955)
XLA Ops:
  0.6 86.6 %gradients.1 = (bf16[128,256]{1,0:T(8,128)(2,1)}, bf16[128,512]{1,0:T(8,128)(2,1)}, bf16[2,256,512]{2,1,0:T(8,128)(2,1)}, bf16[2,4,32,512]{3,2,1,0:T(8,128)(2,1)...) custom-call(bf16[128,256]{1,0:T(8,128)(2,1)} %refs_0_.1, bf16[128,512]{1,0:T(8,128)(2,1)} %refs_1_.1, ...), custom_call_target="tpu_custom_call" | custom-call | flops 2000000000 | bytes 4194304 | tf_op jit(solution)/shard_map/gradients/pallas_call | solution.py:810
  87.2 2.7 %finish.1 = (bf16[128,256]{1,0:T(8,128)(2,1)}, bf16[128,512]{1,0:T(8,128)(2,1)}, f32[2,256,512]{2,1,0:T(8,128)}, f32[256,512]{1,0:T(8,128)}, f32[32,512]{1,0:T(8...) custom-call(bf16[128,256]{1,0:T(8,128)(2,1)} %get-tuple-element.20.refs_0_, bf16[128,512]{1,0:T(8,128)(2,1)} %get-tuple-element.21.refs_1_, ...), custom_call_target="tpu_custom_call" | custom-call | flops 1000000 | bytes 4194304 | tf_op jit(solution)/shard_map/finish/pallas_call | solution.py:810

commit v6 on v5

--- a/solution.py
+++ b/solution.py
@@ -366,14 +366,24 @@
         if kept is not None:
             r.hh[pl.ds(at + r.N, r.N), :] = h
             kept[pl.ds(t * r.N, r.N), :] = h.astype(BF16)
+            r.hb[pl.ds(at, r.N), :] = h.astype(BF16)
     return h
 
 
 def forward_sums(r, j, kept, mask):
     rows = pl.ds(pl.multiple_of(j * CH, CH), CH)
     states = kept[...]
-    r.y_scan[rows, :] = dot(r.cd[rows, :], states)
     r.cm[rows, :] = mask * contract_last(r.g[rows, :].astype(BF16), states)
+
+
+def outputs(r):
+    def one(j, carry):
+        rows = pl.ds(pl.multiple_of(j * CH, CH), CH)
+        states = r.hb[pl.ds(pl.multiple_of(j * CH * r.N, CH * r.N), CH * r.N), :]
+        r.y_scan[rows, :] = dot(r.cd[rows, :], states)
+        return carry
+
+    lax.fori_loop(0, r.T // CH, one, 0)
 
 
 def forward_free(r):
@@ -465,6 +475,8 @@
     r.bd[...] = (tall * dot(r.bcw[:, pl.ds(0, r.N)], picked)).astype(BF16)
     r.cd[...] = (tall * dot(r.bcw[:, pl.ds(r.N, r.N)], picked)).astype(BF16)
 
+    r.sp[...] = jax.nn.sigmoid(r.pre[...])
+
     def enter(j, into):
         rcopy(r.sd, r.sd_r.at[j], r.sems[b.sd_s].at[0], r.sems[b.sd_r].at[j], j, r.c).wait_recv()
         state_copy(r, 0, j, j).wait_recv()
@@ -483,7 +495,7 @@
     a_adj = backward_full(r)
     s1 = r.s1[...]
     u = r.u[...].astype(F32)
-    pre_adj = ((u * s1 + r.s2[...]) * jax.nn.sigmoid(r.pre[...])).astype(BF16)
+    pre_adj = ((u * s1 + r.s2[...]) * r.sp[...]).astype(BF16)
     exact = lax.Precision.HIGHEST
     nt = (((1,), (1,)), ((), ()))
     b_adj = lax.dot_general(r.bm[...], picked, nt, precision=exact, preferred_element_type=F32)
@@ -500,6 +512,7 @@
     start(r, pair_copy(r, r.mi_p.at[1 - r.k], r.mi_b, b.m1))
     skip = r.skip_d[...]
     r.uu[...] = r.delta[...] * s1 + skip * r.g[...]
+    outputs(r)
     r.gate_out[...] = (r.gs[...] * (r.y_scan[...] + skip * u)).astype(BF16)
 
 
@@ -567,12 +580,14 @@
     for i in range(1, r.nY):
         start(r, line_copy(r, i, r.mi_c.at[r.y], r.mi_c.at[r.y], b.m2, r.y))
     recv_wait(r, b.chan, r.part2_a, b.p4)
-    full = jnp.concatenate(unpack(r, r.part2_a[...]), 1).astype(BF16)
-    r.lg[r.y] = full
+    low_adj, bc_adj = unpack(r, r.part2_a[...])
+    low_adj = low_adj.astype(BF16)
+    r.lg[r.y] = low_adj
+    r.bt[r.y] = bc_adj.T[: 2 * r.N].astype(BF16)
     for i in range(1, r.nY):
         start(r, line_copy(r, i, r.lg.at[r.y], r.lg.at[r.y], b.lg, r.y))
-    low_adj = full[:, : r.R]
-    bc_adj = full[:, r.R : r.R + 2 * r.N]
+        start(r, line_copy(r, i, r.bt.at[r.y], r.bt.at[r.y], b.bt, r.y))
+    bc_adj = bc_adj[:, : 2 * r.N].astype(BF16)
     u_adj = r.uu[...] + dot(low_adj, r.w_delta_in[...]) + dot(bc_adj, r.w_bc[...])
     conv_adj = u_adj * r.slope[...]
     r.cpad[pl.ds(0, r.T), :] = conv_adj
@@ -631,25 +646,35 @@
         y2 = lax.rem(r.y + i, r.nY)
         line_copy(r, i, r.ug.at[y2], r.ug.at[y2], b.ug, y2).wait_recv()
         line_copy(r, i, r.lg.at[y2], r.lg.at[y2], b.lg, y2).wait_recv()
+        line_copy(r, i, r.bt.at[y2], r.bt.at[y2], b.bt, y2).wait_recv()
     tokens = r.nY * r.T
-    term = contract_first(r.lg[...].reshape(tokens, r.R + LANES), r.ug[...].reshape(tokens, r.C))
-    r.li_p[...] = term[: r.R + 2 * r.N].astype(BF16)
+    term = contract_first(r.lg[...].reshape(tokens, r.R), r.ug[...].reshape(tokens, r.C))
+    r.li_p[pl.ds(0, r.R), :] = term.astype(BF16)
+    term = dot(r.bt[0], r.ug[0])
+    for y2 in range(1, r.nY):
+        term = term + dot(r.bt[y2], r.ug[y2])
+    r.li_p[pl.ds(r.R, 2 * r.N), :] = term.astype(BF16)
     start(r, pair_copy(r, r.li_p, r.li_b, b.d5))
-    for i in range(1, r.nY):
-        y2 = lax.rem(r.y + i, r.nY)
-        x_copy(i, y2, 0).wait_recv()
-        x_copy(i, y2, 1).wait_recv()
-
-    x_all = r.xg[...].reshape(r.nY * r.T, r.C)
-
-    def weight(x2):
-        return contract_first(r.hg[x2].reshape(r.nY * r.T, r.DH), x_all)
-
+    def weight(x2, part):
+        rows, count = pl.ds(part * (r.T // 2), r.T // 2), r.nY * r.T // 2
+        left = r.hg[x2, :, rows].reshape(count, r.DH)
+        return contract_first(left, r.xg[:, rows].reshape(count, r.C))
+
+    def arrive(part):
+        for i in range(1, r.nY):
+            x_copy(i, lax.rem(r.y + i, r.nY), part).wait_recv()
+
+    arrive(0)
+    for j in range(r.nX):
+        r.wl[j] = weight(j, 0)
+    arrive(1)
     for j in range(half):
-        r.ws[j] = weight((1 - r.k) * half + j).astype(BF16)
+        x2 = (1 - r.k) * half + j
+        r.ws[j] = (r.wl[x2] + weight(x2, 1)).astype(BF16)
     start(r, pair_copy(r, r.ws, r.wr, b.wg))
     for j in range(half):
-        r.wo[j] = weight(r.k * half + j)
+        x2 = r.k * half + j
+        r.wo[j] = r.wl[x2] + weight(x2, 1)
     pair_copy(r, r.ws, r.wr, b.wg).wait_recv()
     r.w_out[...] = (r.wo[...] + r.wr[...].astype(F32)).astype(BF16)
     weight_end(r, r.dt_e, b.d4)
@@ -684,7 +709,6 @@
 def tables(dim):
     d = types.SimpleNamespace(**dim)
     t, c, n, rows, q = d.T, d.C, d.N, d.R, d.R // d.nS
-    wide_row = rows + LANES
     buffers = dict(
         hg=((d.nX, d.nY, t, d.DH), BF16),
         wf=((d.nY, d.nX, d.DH, c), BF16),
@@ -711,6 +735,8 @@
         sd=((1, c), F32),
         aa=((t * n, c), F32),
         hh=(((t + 1) * n, c), F32),
+        hb=((t * n, c), BF16),
+        sp=((t, c), F32),
         ef=((2, n, c), BF16),
         st_r=((d.nS, n, c), BF16),
         sd_r=((d.nS, 1, c), F32),
@@ -737,7 +763,8 @@
         dt_d=((d.nY, q, c), BF16),
         dt_e=((2, d.nY, q, c), BF16),
         ug=((d.nY, t, c), BF16),
-        lg=((d.nY, t, wide_row), BF16),
+        lg=((d.nY, t, rows), BF16),
+        bt=((d.nY, 2 * n, t), BF16),
         li_p=((rows + 2 * n, c), BF16),
         li_b=((rows + 2 * n, c), BF16),
         li_e=((rows + 2 * n, c), BF16),
@@ -752,6 +779,7 @@
         ws=((d.nX // 2, d.DH, c), BF16),
         wr=((d.nX // 2, d.DH, c), BF16),
         wo=((d.nX // 2, d.DH, c), F32),
+        wl=((d.nX, d.DH, c), F32),
         w_out=((d.nX // 2, d.DH, c), BF16),
         hidden_out=((t, d.DH), BF16),
         gate_out=((t, c), BF16),
@@ -765,7 +793,7 @@
     )
     sems = dict(loc=2, inp=12)
     pairs = (b.tu, b.wp, b.head, b.wg, b.d1, b.d4, b.d5, b.m1, b.m3)
-    lines = (b.xr, b.tail, b.d2, b.d3, b.m2, b.ug, b.lg)
+    lines = (b.xr, b.tail, b.d2, b.d3, b.m2, b.ug, b.lg, b.bt)
     for key in pairs:
         sems[key + "_s"] = sems[key + "_r"] = 1
     for key in lines:

time: 90.1 us -> 89.2 us (0.990)
  no operation moved by 1% of the time
where the time goes in v6:
time: 89.2 us; the launch traced here: 89.1 us
  Pallas kernels  88.4 us (99%)
    pallas_call x2, Pallas kernels, run(): pl.pallas_call(body, out_shape=[jax.ShapeDtypeStruct(*buffers[name]) for...  88.4 us

profile of v6, /device:TPU:1, one launch (start us, length us, event | category | flops | bytes accessed | tf_op | source)
XLA Modules:
  0.0 89.1 jit_solution(14028810230810179916)
XLA Ops:
  0.6 85.7 %gradients.1 = (bf16[128,256]{1,0:T(8,128)(2,1)}, bf16[128,512]{1,0:T(8,128)(2,1)}, bf16[2,256,512]{2,1,0:T(8,128)(2,1)}, bf16[2,4,32,512]{3,2,1,0:T(8,128)(2,1)...) custom-call(bf16[128,256]{1,0:T(8,128)(2,1)} %refs_0_.1, bf16[128,512]{1,0:T(8,128)(2,1)} %refs_1_.1, ...), custom_call_target="tpu_custom_call" | custom-call | flops 2000000000 | bytes 4194304 | tf_op jit(solution)/shard_map/gradients/pallas_call | solution.py:838
  86.4 2.7 %finish.1 = (bf16[128,256]{1,0:T(8,128)(2,1)}, bf16[128,512]{1,0:T(8,128)(2,1)}, f32[2,256,512]{2,1,0:T(8,128)}, f32[256,512]{1,0:T(8,128)}, f32[32,512]{1,0:T(8...) custom-call(bf16[128,256]{1,0:T(8,128)(2,1)} %get-tuple-element.20.refs_0_, bf16[128,512]{1,0:T(8,128)(2,1)} %get-tuple-element.21.refs_1_, ...), custom_call_target="tpu_custom_call" | custom-call | flops 1000000 | bytes 4194304 | tf_op jit(solution)/shard_map/finish/pallas_call | solution.py:838

commit v7 on v6

--- a/solution.py
+++ b/solution.py
@@ -63,10 +63,17 @@
     return r.c, r.nC, lambda j: (r.s, j)
 
 
+def plane_at(r, i):
+    shifts = [(dz, dx) for dz in range(r.nY) for dx in range(r.nX)]
+    shifts.sort(key=lambda s: min(s[0], r.nY - s[0]) + min(s[1], r.nX - s[1]))
+    dz, dx = shifts[i]
+    return lax.rem(r.z + dz, r.nY) * r.nX + lax.rem(r.x + dx, r.nX)
+
+
 def peers(r, group):
     me, n, dev = ring(r, group)
-    for i in range(1, n):
-        j = lax.rem(me + i, n)
+    for i in range(n - 1, 0, -1):
+        j = plane_at(r, i) if group == b.chan else lax.rem(me + i, n)
         yield i, j, dev(j)
 
 
@@ -518,7 +525,7 @@
 
 def grad_copy(r, i, part):
     rows = pl.ds(part * (r.T // 2), r.T // 2)
-    c2 = lax.rem(r.c + i, r.nC)
+    c2 = plane_at(r, i)
     at = part * r.nC
     return rcopy(
         r.hs.at[i, rows], r.hr.at[r.c, rows], r.sems[b.hg_s].at[at + i], r.sems[b.hg_r].at[at + r.c], r.s, c2
@@ -528,7 +535,7 @@
 def grad_part(r, part):
     rows = pl.ds(part * (r.T // 2), r.T // 2)
     for i in range(r.nC - 1, -1, -1):
-        c2 = lax.rem(r.c + i, r.nC)
+        c2 = plane_at(r, i)
         term = contract_last(r.xg[r.y, rows], r.wf[lax.div(c2, r.nX), lax.rem(c2, r.nX)])
         r.hs[i, rows] = term.astype(BF16)
         if i:
@@ -677,6 +684,7 @@
         r.wo[j] = r.wl[x2] + weight(x2, 1)
     pair_copy(r, r.ws, r.wr, b.wg).wait_recv()
     r.w_out[...] = (r.wo[...] + r.wr[...].astype(F32)).astype(BF16)
+    flush(r)
     weight_end(r, r.dt_e, b.d4)
     pair_copy(r, r.mi_e.at[r.k], r.mi_e.at[1 - r.k], b.m3).wait_recv()
     total = r.hs[0].astype(F32)

time: 89.2 us -> 87.9 us (0.985)
  Pallas kernels: 88.4 us -> 87.1 us
    pallas_call x2, Pallas kernels: 88.4 us -> 87.1 us  [run(): pl.pallas_call(body, out_shape=[jax.ShapeDtypeStruct(*buffers[name]) for...]
where the time goes in v7:
time: 87.9 us; the launch traced here: 87.8 us
  Pallas kernels  87.1 us (99%)
    pallas_call x2, Pallas kernels, run(): pl.pallas_call(body, out_shape=[jax.ShapeDtypeStruct(*buffers[name]) for...  87.1 us

profile of v7, /device:TPU:1, one launch (start us, length us, event | category | flops | bytes accessed | tf_op | source)
XLA Modules:
  0.0 87.8 jit_solution(3724760410548429710)
XLA Ops:
  0.6 84.4 %gradients.1 = (bf16[128,256]{1,0:T(8,128)(2,1)}, bf16[128,512]{1,0:T(8,128)(2,1)}, bf16[2,256,512]{2,1,0:T(8,128)(2,1)}, bf16[2,4,32,512]{3,2,1,0:T(8,128)(2,1)...) custom-call(bf16[128,256]{1,0:T(8,128)(2,1)} %refs_0_.1, bf16[128,512]{1,0:T(8,128)(2,1)} %refs_1_.1, ...), custom_call_target="tpu_custom_call" | custom-call | flops 2000000000 | bytes 4194304 | tf_op jit(solution)/shard_map/gradients/pallas_call | solution.py:846
  85.1 2.7 %finish.1 = (bf16[128,256]{1,0:T(8,128)(2,1)}, bf16[128,512]{1,0:T(8,128)(2,1)}, f32[2,256,512]{2,1,0:T(8,128)}, f32[256,512]{1,0:T(8,128)}, f32[32,512]{1,0:T(8...) custom-call(bf16[128,256]{1,0:T(8,128)(2,1)} %get-tuple-element.20.refs_0_, bf16[128,512]{1,0:T(8,128)(2,1)} %get-tuple-element.21.refs_1_, ...), custom_call_target="tpu_custom_call" | custom-call | flops 1000000 | bytes 4194304 | tf_op jit(solution)/shard_map/finish/pallas_call | solution.py:846

commit v8 on v7

--- a/solution.py
+++ b/solution.py
@@ -134,6 +134,10 @@
         lax.rem(r.y + i, r.nY) * 2 + r.k,
         r.c,
     )
+
+
+def far_first(n):
+    return sorted(range(1, n), key=lambda i: -min(i, n - i))
 
 
 def plane_copy(r, i, along_x, src, dst, key, slot):
@@ -246,7 +250,7 @@
         ).wait_recv()
 
     low, high = pl.ds(0, cut), pl.ds(cut, r.T - cut)
-    for i in range(1, r.nX):
+    for i in far_first(r.nX):
         start(r, plane_copy(r, i, True, r.hg.at[r.x, r.z, low], r.hg.at[r.x, r.z, low], b.g1, r.x))
         start(r, plane_copy(r, i, False, r.hg.at[r.x, r.z, high], r.hg.at[r.x, r.z, high], b.g1, r.z))
     weight_send(r, 0)
@@ -254,7 +258,7 @@
         x2, z2 = lax.rem(r.x + i, r.nX), lax.rem(r.z + i, r.nY)
         plane_copy(r, i, True, r.hg.at[x2, r.z, low], r.hg.at[x2, r.z, low], b.g1, x2).wait_recv()
         plane_copy(r, i, False, r.hg.at[r.x, z2, high], r.hg.at[r.x, z2, high], b.g1, z2).wait_recv()
-    for i in range(1, r.nX):
+    for i in far_first(r.nX):
         start(r, plane_copy(r, i, False, r.hg.at[:, r.z, low], r.hg.at[:, r.z, low], b.g2, r.z))
         start(r, plane_copy(r, i, True, r.hg.at[r.x, :, high], r.hg.at[r.x, :, high], b.g2, r.x))
     pair_copy(r, r.w_in, r.wf.at[r.y, pl.ds((1 - r.k) * half, half)], b.wp).wait_recv()
@@ -591,7 +595,7 @@
     low_adj = low_adj.astype(BF16)
     r.lg[r.y] = low_adj
     r.bt[r.y] = bc_adj.T[: 2 * r.N].astype(BF16)
-    for i in range(1, r.nY):
+    for i in far_first(r.nY):
         start(r, line_copy(r, i, r.lg.at[r.y], r.lg.at[r.y], b.lg, r.y))
         start(r, line_copy(r, i, r.bt.at[r.y], r.bt.at[r.y], b.bt, r.y))
     bc_adj = bc_adj[:, : 2 * r.N].astype(BF16)
@@ -627,7 +631,7 @@
         return line_copy(r, i, r.xg.at[slot, rows], r.xg.at[slot, rows], b.xg, slot, part)
 
     x_adj(0, r.T // 2)
-    for i in range(1, r.nY):
+    for i in far_first(r.nY):
         start(r, x_copy(i, r.y, 0))
     for part in range(2):
         for i in range(1, r.nY):
@@ -636,7 +640,7 @@
     weight_line(r, r.dt_c, r.dt_d, r.dt_e, (b.d2, b.d3))
     pl.when(r.s < r.nS - 1)(lambda: head_copy(r.s + 1).wait_recv())
     x_adj(r.T // 2, r.T // 2)
-    for i in range(1, r.nY):
+    for i in far_first(r.nY):
         start(r, x_copy(i, r.y, 1))
     grad_part(r, 1)
     total = None

time: 87.9 us -> 88.1 us (level)
  no operation moved by 1% of the time
where the time goes in v8:
time: 88.1 us; the launch traced here: 88 us
  Pallas kernels  87.3 us (99%)
    pallas_call x2, Pallas kernels, run(): pl.pallas_call(body, out_shape=[jax.ShapeDtypeStruct(*buffers[name]) for...  87.3 us

profile of v8, /device:TPU:1, one launch (start us, length us, event | category | flops | bytes accessed | tf_op | source)
XLA Modules:
  0.0 88.0 jit_solution(11452468432577026918)
XLA Ops:
  0.6 84.6 %gradients.1 = (bf16[128,256]{1,0:T(8,128)(2,1)}, bf16[128,512]{1,0:T(8,128)(2,1)}, bf16[2,256,512]{2,1,0:T(8,128)(2,1)}, bf16[2,4,32,512]{3,2,1,0:T(8,128)(2,1)...) custom-call(bf16[128,256]{1,0:T(8,128)(2,1)} %refs_0_.1, bf16[128,512]{1,0:T(8,128)(2,1)} %refs_1_.1, ...), custom_call_target="tpu_custom_call" | custom-call | flops 2000000000 | bytes 4194304 | tf_op jit(solution)/shard_map/gradients/pallas_call | solution.py:850
  85.2 2.7 %finish.1 = (bf16[128,256]{1,0:T(8,128)(2,1)}, bf16[128,512]{1,0:T(8,128)(2,1)}, f32[2,256,512]{2,1,0:T(8,128)}, f32[256,512]{1,0:T(8,128)}, f32[32,512]{1,0:T(8...) custom-call(bf16[128,256]{1,0:T(8,128)(2,1)} %get-tuple-element.20.refs_0_, bf16[128,512]{1,0:T(8,128)(2,1)} %get-tuple-element.21.refs_1_, ...), custom_call_target="tpu_custom_call" | custom-call | flops 1000000 | bytes 4194304 | tf_op jit(solution)/shard_map/finish/pallas_call | solution.py:850
